TPU v7x, 512 devices: a whole 4x8x8 slice. The times are simulated.
512 devices in a mesh: gx: 128 (over x, z, y_lo, core), gy: 4 (over y_hi).
Axes of the slice: x: 4, y: 8 (y_hi: 4, y_lo: 2; y = y_hi * 2 + y_lo), z: 8, core: 2. Of those that a mesh axis runs over, the one named last changes fastest.
Arguments:
- gas_state: float32 [14, 1536, 1024], P(None, 'gx', 'gy'), may hold values from -2 to 8, as said below
- inflow: float32 [14, 1024], P(None, 'gy'), may hold values from -2 to 8, as said below
- slide_count: int32 [1], replicated, may hold values from 1 to 6
- cut_list: int32 [129], replicated, may hold values from 0 to 1536, as said below
- prefactor: float32 [8], replicated, may hold values from 4 to 40
- activation: float32 [8], replicated, may hold values from 1 to 4
- heat_release: float32 [8], replicated, may hold values from 2 to 8
Outputs:
- slabs: float32 [14, 1920, 1024], P(None, 'gx', 'gy')
Inputs may be any that keep to these rules, and one draw needn't show every extreme that they name: `gas_state`: conserved variables of a gas with density between 0.5 and 2, pressure between 0.8 and 2, each velocity component between -0.6 and 0.6, and mass fractions summing to one. `inflow`: conserved variables of a gas with density between 0.5 and 2, pressure between 0.8 and 2, each velocity component between -0.6 and 0.6, and mass fractions summing to one. cut_list[0] = 0, cut_list[128] = 1536, increasing; every slab has 9 to 15 planes, exactly 15 on some device; cut_list[i] differs from i * 12 by at most 3.
All inputs are finite; a program needn't handle non-finite values.
Results may differ from a plain program's by a relative error of at most 0.00002.
Values sent between devices are 32-bit elements; how exact they have to be, the bound alone decides.
A program may use at most 64 MiB of HBM per device.

v0:
```python
import jax
import jax.numpy as jnp
from jax import lax
from jax.sharding import PartitionSpec as P

NZ = 32


GAS_GAMMA = 1.4
TIME_STEP = 0.025


def passed_along(shard, axis, by):
    size = lax.axis_size(axis)
    pairs = [(i, i + by) for i in range(size) if 0 <= i + by < size]
    return lax.ppermute(shard, axis, pairs)


def with_halo(shard, sides, width):
    for axis, dim in sides:
        size, length = (lax.axis_size(axis), shard.shape[dim])
        up = [(i, (i + 1) % size) for i in range(size - 1)]
        down = [(j, i) for i, j in up]
        last = lax.slice_in_dim(shard, length - width, length, axis=dim)
        initial = lax.slice_in_dim(shard, 0, width, axis=dim)
        before = lax.ppermute(last, axis, up)
        after = lax.ppermute(initial, axis, down)
        shard = jnp.concatenate([before, shard, after], axis=dim)
    return shard


def to_primitive(conserved):
    density = conserved[0]
    velocity = conserved[1:4] / density
    kinetic = 0.5 * density * jnp.sum(velocity * velocity, axis=0)
    pressure = (GAS_GAMMA - 1.0) * (conserved[4] - kinetic)
    fractions = conserved[5:] / density
    return jnp.concatenate([density[None], velocity, pressure[None], fractions], axis=0)


def reconstruct(values, axis, extent):
    stencil = [
        lax.slice_in_dim(values, offset, offset + extent + 1, axis=axis) for offset in range(6)
    ]
    upwind_low = (
        2.0 * stencil[0]
        - 13.0 * stencil[1]
        + 47.0 * stencil[2]
        + 27.0 * stencil[3]
        - 3.0 * stencil[4]
    ) / 60.0
    upwind_high = (
        -3.0 * stencil[1]
        + 27.0 * stencil[2]
        + 47.0 * stencil[3]
        - 13.0 * stencil[4]
        + 2.0 * stencil[5]
    ) / 60.0
    return (upwind_low, upwind_high)


def physical(values, direction):
    density = values[0]
    velocity = values[1:4]
    pressure = values[4]
    fractions = values[5:]
    normal = velocity[direction]
    energy = pressure / (GAS_GAMMA - 1.0) + 0.5 * density * jnp.sum(velocity * velocity, axis=0)
    conserved = jnp.concatenate(
        [density[None], density * velocity, energy[None], density * fractions], axis=0
    )
    fluxes = conserved * normal
    fluxes = fluxes.at[1 + direction].add(pressure)
    fluxes = fluxes.at[4].add(pressure * normal)
    wave_speed = jnp.abs(normal) + jnp.sqrt(GAS_GAMMA * pressure / density)
    return (conserved, fluxes, wave_speed)


def divergence(padded, axis, direction):
    extent = padded.shape[axis] - 6
    upwind_low, upwind_high = reconstruct(to_primitive(padded), axis, extent)
    cons_low, flux_low, speed_low = physical(upwind_low, direction)
    cons_high, flux_high, speed_high = physical(upwind_high, direction)
    fluxes = 0.5 * (flux_low + flux_high) - 0.5 * jnp.maximum(speed_low, speed_high) * (
        cons_high - cons_low
    )
    return lax.slice_in_dim(fluxes, 1, extent + 1, axis=axis) - lax.slice_in_dim(
        fluxes, 0, extent, axis=axis
    )


def chemistry(primitive, prefactor, activation, heat_release):
    density = primitive[0]
    pressure = primitive[4]
    fractions = primitive[5:]
    reaction_rates = (
        prefactor.reshape(-1, 1, 1, 1)
        * density
        * fractions[:-1]
        * jnp.exp(-activation.reshape(-1, 1, 1, 1) * density / pressure)
    )
    species = jnp.concatenate(
        [-reaction_rates[:1], reaction_rates[:-1] - reaction_rates[1:], reaction_rates[-1:]], axis=0
    )
    release = jnp.sum(heat_release.reshape(-1, 1, 1, 1) * reaction_rates, axis=0)
    no_source = jnp.zeros((4,) + density.shape, density.dtype)
    return jnp.concatenate([no_source, release[None], species], axis=0)


def tendency(x_padded, y_padded, interior, prefactor, activation, heat_release):
    z_padded = jnp.concatenate([interior[..., -3:], interior, interior[..., :3]], axis=3)
    total = divergence(x_padded, 1, 0) + divergence(y_padded, 2, 1) + divergence(z_padded, 3, 2)
    return chemistry(to_primitive(interior), prefactor, activation, heat_release) - total


def mirror(edge_rows):
    wall_sign = (
        jnp.where(jnp.arange(edge_rows.shape[0]) == 2, -1.0, 1.0)
        .astype(edge_rows.dtype)
        .reshape(-1, 1, 1, 1)
    )
    return jnp.flip(edge_rows, axis=2) * wall_sign


def body(gas_state, inflow, slide_count, cut_list, prefactor, activation, heat_release):
    variables, planes, flat_cells = gas_state.shape
    row_cells = flat_cells // NZ
    balance = planes // 4
    capacity = planes + balance
    half_slab = planes // 2
    slab_index = lax.axis_index("gx")
    is_last = slab_index == lax.axis_size("gx") - 1
    row_index = lax.axis_index("gy")
    last_row = lax.axis_size("gy") - 1
    slide = slide_count[0]
    first_plane = cut_list[slab_index]
    plane_count = cut_list[slab_index + 1] - first_plane
    offset = first_plane - slab_index * planes
    fresh_gas = inflow[:, None, :]
    depth = 3
    rim = balance + depth

    def fresh_planes(count):
        return jnp.broadcast_to(fresh_gas, (variables, count, flat_cells))

    ahead = passed_along(gas_state[:, :half_slab], "gx", -1)
    ahead = jnp.where(is_last, fresh_planes(half_slab), ahead)
    slid_slab = lax.dynamic_slice_in_dim(
        jnp.concatenate([gas_state, ahead], axis=1), slide, planes, 1
    )
    behind = passed_along(slid_slab[:, planes - rim :], "gx", 1)
    beyond = passed_along(slid_slab[:, :rim], "gx", -1)
    joined = jnp.concatenate([behind, slid_slab, beyond, fresh_planes(rim)], axis=1)
    widened = lax.dynamic_slice_in_dim(joined, offset + balance, capacity + 2 * depth, 1)
    slab = widened[:, depth : depth + capacity]
    given_ghosts = (widened[:, :3], lax.dynamic_slice_in_dim(widened, plane_count + 3, 3, 1))
    is_valid = (jnp.arange(capacity, dtype=jnp.int32) < plane_count)[None, :, None]
    slab = jnp.where(is_valid, slab, fresh_planes(capacity))

    def advance_rate(cell_values, ghosts):
        if ghosts is None:
            edge_low = cell_values[:, :3]
            edge_high = lax.dynamic_slice_in_dim(cell_values, plane_count - 3, 3, 1)
            ghost_low = passed_along(edge_high, "gx", 1)
            ghost_high = passed_along(edge_low, "gx", -1)
        else:
            ghost_low, ghost_high = ghosts
        ghost_low = jnp.where(slab_index == 0, jnp.repeat(cell_values[:, :1], 3, axis=1), ghost_low)
        ghost_high = jnp.where(is_last, fresh_planes(3), ghost_high)
        x_padded = jnp.concatenate([ghost_low, cell_values, fresh_planes(3)], axis=1)
        x_padded = lax.dynamic_update_slice_in_dim(x_padded, ghost_high, plane_count + 3, 1)
        y_flat = with_halo(cell_values, (("gy", 2),), 3 * NZ)
        y_padded = y_flat.reshape(variables, capacity, row_cells + 6, NZ)
        interior = cell_values.reshape(variables, capacity, row_cells, NZ)
        y_padded = jnp.concatenate(
            [
                jnp.where(row_index == 0, mirror(interior[:, :, :3]), y_padded[:, :, :3]),
                y_padded[:, :, 3:-3],
                jnp.where(row_index == last_row, mirror(interior[:, :, -3:]), y_padded[:, :, -3:]),
            ],
            axis=2,
        )
        x_padded = x_padded.reshape(variables, capacity + 6, row_cells, NZ)
        result = tendency(x_padded, y_padded, interior, prefactor, activation, heat_release)
        return result.reshape(variables, capacity, flat_cells)

    segment_one = jnp.where(
        is_valid, slab + TIME_STEP * advance_rate(slab, given_ghosts), fresh_planes(capacity)
    )
    segment_two = 0.75 * slab + 0.25 * (segment_one + TIME_STEP * advance_rate(segment_one, None))
    return jnp.where(is_valid, segment_two, jnp.zeros_like(segment_two))


def solution(mesh):
    in_specs = (P(None, "gx", "gy"), P(None, "gy"), P(), P(), P(), P(), P())
    out_specs = P(None, "gx", "gy")
    return jax.shard_map(body, mesh=mesh, in_specs=in_specs, out_specs=out_specs, check_vma=False)
```

profile of v0, /device:TPU:38, one launch (start us, length us, event | category | flops | bytes accessed | tf_op | source)
XLA Modules:
  0.0 133.3 jit_solution(9548557945755065951)
XLA Ops:
  0.9 10.8 %collective-permute-start = (f32[14,6,256]{2,0,1:T(8,128)S(1)}, f32[14,6,256]{2,0,1:T(8,128)S(1)}, u32[]{:S(2)}, u32[]{:S(2)}) collective-permute-start(f32[14,6,256]{2,0,1:T(8,128)S(1)} %slice.1224), channel_id=1, source_target_pairs={{4,0},{8,4},{12,8},{16,12},{20,16},{24,20},{28,24},{32,28},{36,32}... | collective-permute-start | bytes 258056 | tf_op jit(solution)/shard_map/ppermute | solution.py:16
  12.4 1.4 %fusion.135 = (s32[1]{0:T(128)}, s32[1]{0:T(128)}) fusion(s32[129]{0:T(256)} %param.58, s32[]{:T(128)S(6)} %select_n.103, s32[]{:T(128)S(6)} %select_n.104), kind=kLoop, calls=%fused_computation.367 | loop fusion | bytes 24 | tf_op jit(solution)/shard_map/dynamic_slice | solution.py:137
  17.2 1.2 neg.11
  20.1 1.9 %collective-permute-start.1 = (f32[14,6,256]{2,0,1:T(8,128)S(1)}, f32[14,6,256]{2,0,1:T(8,128)S(1)}, u32[]{:S(2)}, u32[]{:S(2)}) collective-permute-start(f32[14,6,256]{2,0,1:T(8,128)S(1)} %get-tuple-element.405), channel_id=1, source_target_pairs={{0,4},{4,8},{8,12},{12,16},{16,20},{20,24},{24,28},{28,32},{32,36}... | collective-permute-start | bytes 258056 | tf_op jit(solution)/shard_map/ppermute | solution.py:16
  22.0 6.7 %collective-permute-start.2 = (f32[14,6,256]{2,0,1:T(8,128)S(1)}, f32[14,6,256]{2,0,1:T(8,128)S(1)}, u32[]{:S(2)}, u32[]{:S(2)}) collective-permute-start(f32[14,6,256]{2,0,1:T(8,128)S(1)} %get-tuple-element.406), channel_id=1, source_target_pairs={{4,0},{8,4},{12,8},{16,12},{20,16},{24,20},{28,24},{32,28},{36,32}... | collective-permute-start | bytes 258056 | tf_op jit(solution)/shard_map/ppermute | solution.py:16
  29.6 1.3 collective-permute-done.2
  37.8 1.2 reshape.982
  39.0 1.1 fusion.127
  41.2 1.2 fusion.49
  45.4 2.7 %collective-permute-start.3 = (f32[14,15,96]{2,0,1:T(8,128)}, f32[14,15,96]{2,0,1:T(8,128)}, u32[]{:S(2)}, u32[]{:S(2)}) collective-permute-start(f32[14,15,96]{2,0,1:T(8,128)} %get-tuple-element.402), channel_id=1, source_target_pairs={{0,1},{1,2},{2,3},{4,5},{5,6},{6,7},{8,9},{9,10},{10,11},{12,13},{... | collective-permute-start | bytes 241928 | tf_op jit(solution)/shard_map/ppermute | solution.py:26
  48.1 5.4 %collective-permute-start.4 = (f32[14,15,96]{2,0,1:T(8,128)}, f32[14,15,96]{2,0,1:T(8,128)}, u32[]{:S(2)}, u32[]{:S(2)}) collective-permute-start(f32[14,15,96]{2,0,1:T(8,128)} %get-tuple-element.403), channel_id=1, source_target_pairs={{1,0},{2,1},{3,2},{5,4},{6,5},{7,6},{9,8},{10,9},{11,10},{13,12},{... | collective-permute-start | bytes 241928 | tf_op jit(solution)/shard_map/ppermute | solution.py:27
  56.5 1.1 multiply_reduce_fusion.1
  63.4 1.6 %rev.14 = f32[14,15,3,32]{3,2,1,0:T(4,128)S(1)} reverse(f32[14,15,3,32]{3,2,1,0:T(4,128)} %get-tuple-element.377), dimensions={2} | reverse | bytes 161280 | tf_op jit(solution)/shard_map/jit(_flip)/rev | solution.py:122
  65.0 1.2 pad_maximum_fusion.29
  66.5 1.8 %reshape.983 = f32[14,15,14,32]{3,2,1,0:T(8,128)} reshape(f32[14,15,448]{2,1,0:T(8,128)S(1)} %copy.35) | data formatting | bytes 752640 | tf_op jit(solution)/shard_map/reshape | solution.py:173
  68.2 1.7 %slice.1476 = f32[14,15,8,32]{3,2,1,0:T(8,128)S(1)} slice(f32[14,15,14,32]{3,2,1,0:T(8,128)} %reshape.983), slice={[0:14], [0:15], [3:11], [0:32]} | slice | bytes 430080 | tf_op jit(solution)/shard_map/slice | solution.py:178
  71.2 1.7 %fusion.8 = (f32[14,15,9,32]{3,2,1,0:T(8,128)S(1)}, f32[14,15,9,32]{3,2,1,0:T(8,128)S(1)}) fusion(f32[14,15,14,32]{3,2,1,0:T(8,128)S(1)} %pad_maximum_fusion), kind=kLoop, calls=%fused_computation.11 | loop fusion | flops 1209600 | bytes 1935360 | tf_op jit(solution)/shard_map/div | solution.py:52
  79.4 1.2 fusion.38
  81.6 1.2 slice_reduce_fusion.4
  83.4 1.9 %collective-permute-start.5 = (f32[14,3,256]{2,0,1:T(8,128)}, f32[14,3,256]{2,0,1:T(8,128)}, u32[]{:S(2)}, u32[]{:S(2)}) collective-permute-start(f32[14,3,256]{2,0,1:T(8,128)} %get-tuple-element.398), channel_id=1, source_target_pairs={{0,4},{4,8},{8,12},{12,16},{16,20},{20,24},{24,28},{28,32},{32,36}... | collective-permute-start | bytes 129032 | tf_op jit(solution)/shard_map/ppermute | solution.py:16
  85.4 2.1 %collective-permute-start.7 = (f32[14,15,96]{2,0,1:T(8,128)}, f32[14,15,96]{2,0,1:T(8,128)}, u32[]{:S(2)}, u32[]{:S(2)}) collective-permute-start(f32[14,15,96]{2,0,1:T(8,128)} %get-tuple-element.399), channel_id=1, source_target_pairs={{0,1},{1,2},{2,3},{4,5},{5,6},{6,7},{8,9},{9,10},{10,11},{12,13},{... | collective-permute-start | bytes 241928 | tf_op jit(solution)/shard_map/ppermute | solution.py:26
  88.7 1.9 %slice.1333 = f32[9,15,8,32]{3,2,1,0:T(8,128)} reshape(f32[9,15,256]{2,1,0:T(8,128)} %copy.37) | data formatting | bytes 276480 | tf_op jit(solution)/shard_map/slice | solution.py:37
  92.0 1.4 %reduce_sum.260 = f32[15,8,32]{2,1,0:T(8,128)} reshape(f32[15,256]{1,0:T(8,128)} %fusion.122) | data formatting | bytes 30720 | tf_op jit(solution)/shard_map/reduce_sum | solution.py:35
  93.4 1.4 %mul.1314 = f32[15,8,32]{2,1,0:T(8,128)} reshape(f32[15,256]{1,0:T(8,128)} %get-tuple-element.297) | data formatting | bytes 30720 | tf_op jit(solution)/shard_map/mul | solution.py:97
  96.6 1.4 %multiply_reduce_fusion = (f32[15,8,32]{2,1,0:T(8,128)S(1)}, f32[8,15,8,32]{3,2,1,0:T(8,128)S(1)}) fusion(f32[8]{0:T(128)S(1)} %copy-done.73, f32[15,8,32]{2,1,0:T(8,128)S(1)} %subtract_multiply_fusion.2, f32[8]{0:T(128)S(1)} %copy-done.75, f32[9,15,8,32]{3,2,1,0:T(8,128)} %slice.1333, f32[15,8,32]{2,1,0:T(8,128)} %mul.1314, f32[8]{0:T(128)S(1)} %copy-done.74), kind=kLoop, calls=%fused_computation.139 | loop fusion | flops 241920 | bytes 291936 | tf_op jit(solution)/shard_map/reduce_sum | solution.py:105
  101.0 6.6 %collective-permute-start.6 = (f32[14,3,256]{2,0,1:T(8,128)}, f32[14,3,256]{2,0,1:T(8,128)S(1)}, u32[]{:S(2)}, u32[]{:S(2)}) collective-permute-start(f32[14,3,256]{2,0,1:T(8,128)} %get-tuple-element.397), channel_id=1, source_target_pairs={{4,0},{8,4},{12,8},{16,12},{20,16},{24,20},{28,24},{32,28},{36,32}... | collective-permute-start | bytes 129032 | tf_op jit(solution)/shard_map/ppermute | solution.py:16
  107.7 5.8 %collective-permute-start.8 = (f32[14,15,96]{2,0,1:T(8,128)}, f32[14,15,96]{2,0,1:T(8,128)}, u32[]{:S(2)}, u32[]{:S(2)}) collective-permute-start(f32[14,15,96]{2,0,1:T(8,128)} %get-tuple-element.400), channel_id=1, source_target_pairs={{1,0},{2,1},{3,2},{5,4},{6,5},{7,6},{9,8},{10,9},{11,10},{13,12},{... | collective-permute-start | bytes 241928 | tf_op jit(solution)/shard_map/ppermute | solution.py:27
  114.2 1.6 %rev.16 = f32[14,15,3,32]{3,2,1,0:T(4,128)S(1)} reverse(f32[14,15,3,32]{3,2,1,0:T(4,128)} %get-tuple-element.362), dimensions={2} | reverse | bytes 161280 | tf_op jit(solution)/shard_map/jit(_flip)/rev | solution.py:122
  121.0 1.2 pad_maximum_fusion.30
  122.4 1.8 %reshape.986 = f32[14,15,14,32]{3,2,1,0:T(8,128)} reshape(f32[14,15,448]{2,1,0:T(8,128)S(1)} %copy.41) | data formatting | bytes 752640 | tf_op jit(solution)/shard_map/reshape | solution.py:173
  124.2 1.7 %slice.1566 = f32[14,15,8,32]{3,2,1,0:T(8,128)S(1)} slice(f32[14,15,14,32]{3,2,1,0:T(8,128)} %reshape.986), slice={[0:14], [0:15], [3:11], [0:32]} | slice | bytes 430080 | tf_op jit(solution)/shard_map/slice | solution.py:178
  127.2 1.7 %fusion.1 = (f32[14,15,9,32]{3,2,1,0:T(8,128)S(1)}, f32[14,15,9,32]{3,2,1,0:T(8,128)S(1)}) fusion(f32[14,15,14,32]{3,2,1,0:T(8,128)S(1)} %pad_maximum_fusion.3), kind=kLoop, calls=%fused_computation.2 | loop fusion | flops 1209600 | bytes 1935360 | tf_op jit(solution)/shard_map/div | solution.py:52
  (360 shorter events, 52.2 us)
Async XLA Ops:
  0.0 30.9 %copy-start.38 = (f32[14,256]{1,0:T(8,128)S(1)}, f32[14,256]{1,0:T(8,128)}, u32[]{:S(2)}) copy-start(f32[14,256]{1,0:T(8,128)} %param.56) | copy-start | bytes 43012
  0.9 17.5 %collective-permute-start = (f32[14,6,256]{2,0,1:T(8,128)S(1)}, f32[14,6,256]{2,0,1:T(8,128)S(1)}, u32[]{:S(2)}, u32[]{:S(2)}) collective-permute-start(f32[14,6,256]{2,0,1:T(8,128)S(1)} %slice.1224), channel_id=1, source_target_pairs={{4,0},{8,4},{12,8},{16,12},{20,16},{24,20},{28,24},{32,28},{36,32}... | collective-permute-start | bytes 258056 | tf_op jit(solution)/shard_map/ppermute | solution.py:16
  20.1 9.5 %collective-permute-start.1 = (f32[14,6,256]{2,0,1:T(8,128)S(1)}, f32[14,6,256]{2,0,1:T(8,128)S(1)}, u32[]{:S(2)}, u32[]{:S(2)}) collective-permute-start(f32[14,6,256]{2,0,1:T(8,128)S(1)} %get-tuple-element.405), channel_id=1, source_target_pairs={{0,4},{4,8},{8,12},{12,16},{16,20},{20,24},{24,28},{28,32},{32,36}... | collective-permute-start | bytes 258056 | tf_op jit(solution)/shard_map/ppermute | solution.py:16
  22.0 8.8 %collective-permute-start.2 = (f32[14,6,256]{2,0,1:T(8,128)S(1)}, f32[14,6,256]{2,0,1:T(8,128)S(1)}, u32[]{:S(2)}, u32[]{:S(2)}) collective-permute-start(f32[14,6,256]{2,0,1:T(8,128)S(1)} %get-tuple-element.406), channel_id=1, source_target_pairs={{4,0},{8,4},{12,8},{16,12},{20,16},{24,20},{28,24},{32,28},{36,32}... | collective-permute-start | bytes 258056 | tf_op jit(solution)/shard_map/ppermute | solution.py:16
  43.2 10.3 %copy-start.51 = (f32[1,15,8,33]{3,2,1,0:T(8,128)}, f32[1,15,8,33]{3,2,1,0:T(8,128)S(1)}, u32[]{:S(2)}) copy-start(f32[1,15,8,33]{3,2,1,0:T(8,128)S(1)} %get-tuple-element.385) | copy-start | bytes 47524
  43.2 10.4 %copy-start.53 = (f32[1,15,8,33]{3,2,1,0:T(8,128)}, f32[1,15,8,33]{3,2,1,0:T(8,128)S(1)}, u32[]{:S(2)}) copy-start(f32[1,15,8,33]{3,2,1,0:T(8,128)S(1)} %get-tuple-element.386) | copy-start | bytes 47524
  43.2 10.5 %copy-start.47 = (f32[1,15,8,33]{3,2,1,0:T(8,128)}, f32[1,15,8,33]{3,2,1,0:T(8,128)S(1)}, u32[]{:S(2)}) copy-start(f32[1,15,8,33]{3,2,1,0:T(8,128)S(1)} %get-tuple-element.381) | copy-start | bytes 47524
  43.2 10.6 %copy-start.49 = (f32[1,15,8,33]{3,2,1,0:T(8,128)}, f32[1,15,8,33]{3,2,1,0:T(8,128)S(1)}, u32[]{:S(2)}) copy-start(f32[1,15,8,33]{3,2,1,0:T(8,128)S(1)} %get-tuple-element.382) | copy-start | bytes 47524
  43.3 10.3 %copy-start.28 = (f32[3,15,8,33]{3,2,1,0:T(8,128)}, f32[3,15,8,33]{3,2,1,0:T(8,128)S(1)}, u32[]{:S(2)}) copy-start(f32[3,15,8,33]{3,2,1,0:T(8,128)S(1)} %get-tuple-element.411) | copy-start | bytes 142564
  43.3 10.5 %copy-start.30 = (f32[3,15,8,33]{3,2,1,0:T(8,128)}, f32[3,15,8,33]{3,2,1,0:T(8,128)S(1)}, u32[]{:S(2)}) copy-start(f32[3,15,8,33]{3,2,1,0:T(8,128)S(1)} %get-tuple-element.412) | copy-start | bytes 142564
  43.4 10.2 %copy-start.4 = (f32[9,15,8,33]{3,2,1,0:T(8,128)}, f32[9,15,8,33]{3,2,1,0:T(8,128)S(1)}, u32[]{:S(2)}) copy-start(f32[9,15,8,33]{3,2,1,0:T(8,128)S(1)} %get-tuple-element.409) | copy-start | bytes 427684
  43.4 10.4 %copy-start.6 = (f32[9,15,8,33]{3,2,1,0:T(8,128)}, f32[9,15,8,33]{3,2,1,0:T(8,128)S(1)}, u32[]{:S(2)}) copy-start(f32[9,15,8,33]{3,2,1,0:T(8,128)S(1)} %get-tuple-element.410) | copy-start | bytes 427684
  45.0 8.6 %copy-start.8 = (f32[14,16,8,32]{3,2,1,0:T(8,128)}, f32[14,16,8,32]{3,2,1,0:T(8,128)S(1)}, u32[]{:S(2)}) copy-start(f32[14,16,8,32]{3,2,1,0:T(8,128)S(1)} %fusion.97) | copy-start | bytes 688132
  45.3 8.5 %copy-start.10 = (f32[14,16,8,32]{3,2,1,0:T(8,128)}, f32[14,16,8,32]{3,2,1,0:T(8,128)S(1)}, u32[]{:S(2)}) copy-start(f32[14,16,8,32]{3,2,1,0:T(8,128)S(1)} %fusion.99) | copy-start | bytes 688132
  45.4 19.6 %collective-permute-start.3 = (f32[14,15,96]{2,0,1:T(8,128)}, f32[14,15,96]{2,0,1:T(8,128)}, u32[]{:S(2)}, u32[]{:S(2)}) collective-permute-start(f32[14,15,96]{2,0,1:T(8,128)} %get-tuple-element.402), channel_id=1, source_target_pairs={{0,1},{1,2},{2,3},{4,5},{5,6},{6,7},{8,9},{9,10},{10,11},{12,13},{... | collective-permute-start | bytes 241928 | tf_op jit(solution)/shard_map/ppermute | solution.py:26
  48.1 16.9 %collective-permute-start.4 = (f32[14,15,96]{2,0,1:T(8,128)}, f32[14,15,96]{2,0,1:T(8,128)}, u32[]{:S(2)}, u32[]{:S(2)}) collective-permute-start(f32[14,15,96]{2,0,1:T(8,128)} %get-tuple-element.403), channel_id=1, source_target_pairs={{1,0},{2,1},{3,2},{5,4},{6,5},{7,6},{9,8},{10,9},{11,10},{13,12},{... | collective-permute-start | bytes 241928 | tf_op jit(solution)/shard_map/ppermute | solution.py:27
  81.4 6.1 %copy-start.59 = (f32[1,15,8,33]{3,2,1,0:T(8,128)}, f32[1,15,8,33]{3,2,1,0:T(8,128)S(1)}, u32[]{:S(2)}) copy-start(f32[1,15,8,33]{3,2,1,0:T(8,128)S(1)} %get-tuple-element.370) | copy-start | bytes 47524
  81.4 6.1 %copy-start.61 = (f32[1,15,8,33]{3,2,1,0:T(8,128)}, f32[1,15,8,33]{3,2,1,0:T(8,128)S(1)}, u32[]{:S(2)}) copy-start(f32[1,15,8,33]{3,2,1,0:T(8,128)S(1)} %get-tuple-element.371) | copy-start | bytes 47524
  81.4 6.3 %copy-start.55 = (f32[1,15,8,33]{3,2,1,0:T(8,128)}, f32[1,15,8,33]{3,2,1,0:T(8,128)S(1)}, u32[]{:S(2)}) copy-start(f32[1,15,8,33]{3,2,1,0:T(8,128)S(1)} %get-tuple-element.366) | copy-start | bytes 47524
  81.4 6.3 %copy-start.57 = (f32[1,15,8,33]{3,2,1,0:T(8,128)}, f32[1,15,8,33]{3,2,1,0:T(8,128)S(1)}, u32[]{:S(2)}) copy-start(f32[1,15,8,33]{3,2,1,0:T(8,128)S(1)} %get-tuple-element.367) | copy-start | bytes 47524
  81.4 6.1 %copy-start.32 = (f32[3,15,8,33]{3,2,1,0:T(8,128)}, f32[3,15,8,33]{3,2,1,0:T(8,128)S(1)}, u32[]{:S(2)}) copy-start(f32[3,15,8,33]{3,2,1,0:T(8,128)S(1)} %slice_multiply_fusion.32) | copy-start | bytes 142564
  81.5 6.2 %copy-start.34 = (f32[3,15,8,33]{3,2,1,0:T(8,128)}, f32[3,15,8,33]{3,2,1,0:T(8,128)S(1)}, u32[]{:S(2)}) copy-start(f32[3,15,8,33]{3,2,1,0:T(8,128)S(1)} %slice_multiply_fusion.33) | copy-start | bytes 142564
  83.4 32.4 %collective-permute-start.5 = (f32[14,3,256]{2,0,1:T(8,128)}, f32[14,3,256]{2,0,1:T(8,128)}, u32[]{:S(2)}, u32[]{:S(2)}) collective-permute-start(f32[14,3,256]{2,0,1:T(8,128)} %get-tuple-element.398), channel_id=1, source_target_pairs={{0,4},{4,8},{8,12},{12,16},{16,20},{20,24},{24,28},{28,32},{32,36}... | collective-permute-start | bytes 129032 | tf_op jit(solution)/shard_map/ppermute | solution.py:16
  85.4 35.6 %collective-permute-start.7 = (f32[14,15,96]{2,0,1:T(8,128)}, f32[14,15,96]{2,0,1:T(8,128)}, u32[]{:S(2)}, u32[]{:S(2)}) collective-permute-start(f32[14,15,96]{2,0,1:T(8,128)} %get-tuple-element.399), channel_id=1, source_target_pairs={{0,1},{1,2},{2,3},{4,5},{5,6},{6,7},{8,9},{9,10},{10,11},{12,13},{... | collective-permute-start | bytes 241928 | tf_op jit(solution)/shard_map/ppermute | solution.py:26
  87.7 8.9 %copy-start.74 = (f32[8]{0:T(128)S(1)}, f32[8]{0:T(128)}, u32[]{:S(2)}) copy-start(f32[8]{0:T(128)} %param.59) | copy-start | bytes 100
  87.7 8.9 %copy-start.75 = (f32[8]{0:T(128)S(1)}, f32[8]{0:T(128)}, u32[]{:S(2)}) copy-start(f32[8]{0:T(128)} %neg.11) | copy-start | bytes 100
  87.8 7.7 %copy-start.16 = (f32[14,15,8,33]{3,2,1,0:T(8,128)}, f32[14,15,8,33]{3,2,1,0:T(8,128)S(1)}, u32[]{:S(2)}) copy-start(f32[14,15,8,33]{3,2,1,0:T(8,128)S(1)} %fusion.107) | copy-start | bytes 665284
  95.5 5.2 %copy-start.35 = (f32[3,15,8,33]{3,2,1,0:T(8,128)S(1)}, f32[3,15,8,33]{3,2,1,0:T(8,128)}, u32[]{:S(2)}) copy-start(f32[3,15,8,33]{3,2,1,0:T(8,128)} %copy-done.34) | copy-start | bytes 142564
  95.5 5.2 %copy-start.56 = (f32[1,15,8,33]{3,2,1,0:T(8,128)S(1)}, f32[1,15,8,33]{3,2,1,0:T(8,128)}, u32[]{:S(2)}) copy-start(f32[1,15,8,33]{3,2,1,0:T(8,128)} %copy-done.55) | copy-start | bytes 47524
  101.0 15.6 %copy-start.64 = (f32[14,3,256]{2,0,1:T(8,128)S(1)}, f32[14,3,256]{2,0,1:T(8,128)}, u32[]{:S(2)}) copy-start(f32[14,3,256]{2,0,1:T(8,128)} %copy-done.63) | copy-start | bytes 129028
  101.0 15.7 %collective-permute-start.6 = (f32[14,3,256]{2,0,1:T(8,128)}, f32[14,3,256]{2,0,1:T(8,128)S(1)}, u32[]{:S(2)}, u32[]{:S(2)}) collective-permute-start(f32[14,3,256]{2,0,1:T(8,128)} %get-tuple-element.397), channel_id=1, source_target_pairs={{4,0},{8,4},{12,8},{16,12},{20,16},{24,20},{28,24},{32,28},{36,32}... | collective-permute-start | bytes 129032 | tf_op jit(solution)/shard_map/ppermute | solution.py:16
  107.7 13.3 %collective-permute-start.8 = (f32[14,15,96]{2,0,1:T(8,128)}, f32[14,15,96]{2,0,1:T(8,128)}, u32[]{:S(2)}, u32[]{:S(2)}) collective-permute-start(f32[14,15,96]{2,0,1:T(8,128)} %get-tuple-element.400), channel_id=1, source_target_pairs={{1,0},{2,1},{3,2},{5,4},{6,5},{7,6},{9,8},{10,9},{11,10},{13,12},{... | collective-permute-start | bytes 241928 | tf_op jit(solution)/shard_map/ppermute | solution.py:27
  (54 other events, 122.2 us)
where the time goes:
time: 135 us; the launch traced here: 133 us
  local copies, waits for them, and re-layouts  47.1 us (35%)
  starting transfers between devices  43.9 us (33%)
  other arithmetic  36.1 us (27%)
  between operations  4.54 us (3%)
  waiting for transfers between devices  1.67 us (1%)
    ppermute x5, starting transfers between devices, passed_along(): return lax.ppermute(shard, axis, pairs)  27.9 us
    ppermute x2, starting transfers between devices, with_halo(): after = lax.ppermute(initial, axis, down)  11.2 us
    unnamed x162, local copies, waits for them, and re-layouts  10 us
    div x6, other arithmetic, reconstruct(): (-3.0 * stencil[1] + 27.0 * stencil[2] + 47.0 * stencil[3] - 13.0 * stenc...  6.93 us
    slice x12, local copies, waits for them, and re-layouts, to_primitive(): fractions = conserved[5:] / density  5.47 us
    ppermute x2, starting transfers between devices, with_halo(): before = lax.ppermute(last, axis, up)  4.85 us
    rev x4, local copies, waits for them, and re-layouts, mirror(): return jnp.flip(edge_rows, axis=2) * wall_sign  4.72 us
    reshape x2, local copies, waits for them, and re-layouts, advance_rate(): y_padded = y_flat.reshape(variables, capacity, row_cells + 6, NZ)  3.53 us
  transfers between devices with their start and end apart: 9, of which 2 were waited for; matrix products, arithmetic and copies ran while one was open for 25% of the time, Pallas kernels for 0%

commit v1 on v0

v1 whole, which is shorter than its diff:
```python
import functools

import jax
import jax.numpy as jnp
from jax import lax
from jax.experimental import pallas as pl
from jax.experimental.pallas import tpu as pltpu
from jax.sharding import PartitionSpec as P

MESH = pl.DeviceIdType.MESH
NV = 14
NR = 8
PX = 12
CAP = 15
NZ = 32
GAS_GAMMA = 1.4
TIME_STEP = 0.025

OWN = 8 * NV
NEXT = OWN + PX * NV
Y_OWN = 4 * NV
Y_NEXT = Y_OWN + PX * NV
V_OWN = 4 * NV
G_OWN = 12 * NV

W_ROWS = 560
Y_ROWS = 424
V_ROWS = 56 + 24 * NV
G_ROWS = 352

LOW = (2.0, -13.0, 47.0, 27.0, -3.0, 0.0)
HIGH = (0.0, -3.0, 27.0, 47.0, -13.0, 2.0)


def stencil_pair(q):
    d = [c / 60.0 for c in (2.0, 13.0, 47.0, 27.0, 3.0)]
    low = (d[0] * q[0] - d[1] * q[1]) + (d[2] * q[2] + d[3] * q[3]) - d[4] * q[4]
    high = (d[3] * q[2] - d[4] * q[1]) + (d[2] * q[3] - d[1] * q[4]) + d[0] * q[5]
    return low, high


def wave_speed(normal, pressure, density):
    scaled = GAS_GAMMA * pressure
    return jnp.abs(normal) + jnp.abs(scaled) * lax.rsqrt(jnp.maximum(scaled * density, 1e-30))


def face_flux(low, high, direction):
    rho_l, rho_r, p_l, p_r = low(0), high(0), low(4), high(4)
    u_l = [low(1 + j) for j in range(3)]
    u_r = [high(1 + j) for j in range(3)]
    n_l, n_r = u_l[direction], u_r[direction]
    speed = jnp.maximum(wave_speed(n_l, p_l, rho_l), wave_speed(n_r, p_r, rho_r))
    a_l, a_r = 0.5 * (n_l + speed), 0.5 * (n_r - speed)
    m_l, m_r = rho_l * a_l, rho_r * a_r
    flux = [m_l + m_r]
    for j in range(3):
        f = m_l * u_l[j] + m_r * u_r[j]
        if j == direction:
            f = f + 0.5 * (p_l + p_r)
        flux.append(f)
    k_l = u_l[0] * u_l[0] + u_l[1] * u_l[1] + u_l[2] * u_l[2]
    k_r = u_r[0] * u_r[0] + u_r[1] * u_r[1] + u_r[2] * u_r[2]
    flux.append(
        p_l * (2.5 * a_l + 0.5 * n_l) + p_r * (2.5 * a_r + 0.5 * n_r) + 0.5 * (m_l * k_l + m_r * k_r)
    )
    for j in range(5, NV):
        flux.append(m_l * low(j) + m_r * high(j))
    return flux


def primitives(c):
    inverse = 1.0 / c[0]
    u = [c[j] * inverse for j in (1, 2, 3)]
    kinetic = 0.5 * (c[1] * u[0] + c[2] * u[1] + c[3] * u[2])
    return [c[0]] + u + [0.4 * (c[4] - kinetic)] + [c[j] * inverse for j in range(5, NV)]


def lane():
    return lax.broadcasted_iota(jnp.int32, (8, 128), 1)


def fill_weights(weights):
    a = lax.broadcasted_iota(jnp.int32, (128, 128), 0)
    b = lax.broadcasted_iota(jnp.int32, (128, 128), 1)
    ga, gb, za, zb = a // NZ, b // NZ, a % NZ, b % NZ
    for slot in range(4):
        if slot == 3:
            offset = jnp.where(ga == gb, (za - zb + 3 + NZ) % NZ, NZ)
        else:
            offset = jnp.where(za == zb, 4 * (slot - 1) + ga - gb + 3, NZ)
        for side, coefficients in enumerate((LOW, HIGH)):
            w = jnp.zeros((128, 128), jnp.float32)
            for m, c in enumerate(coefficients):
                if c:
                    w = jnp.where(offset == m, c, w)
            w = w.astype(jnp.bfloat16)
            weights[slot, 0:128, 128 * side : 128 * side + 128] = w
            weights[slot, 128:256, 128 * side : 128 * side + 128] = w


def split_tile(q, qb, t):
    x = q[:, t, 3:19, :].reshape(NV * 16, 128) * (1.0 / 60.0)
    top = x.astype(jnp.bfloat16)
    qb[t, :, 0:128] = top
    qb[t, :, 128:256] = (x - top.astype(jnp.float32)).astype(jnp.bfloat16)


def dot(a, b):
    return jnp.dot(a, b, preferred_element_type=jnp.float32)


def store_primitives(q, t, row, c):
    for v, value in enumerate(primitives(c)):
        q[v, t, row : row + 8, :] = value


def inner_terms(q, qb, fs, fx, s, weights, rate):
    pre, act, heat = rate
    for t in (1, 2):
        split_tile(q, qb, t)
        fs[t - 1] = dot(qb[t], weights[3])
    first = lane() % NZ == NZ - 1

    def half(h, _):
        for kt in range(2):
            rows = slice(8 * kt, 8 * kt + 8)
            cells = slice(8 * kt + 3, 8 * kt + 11)
            stencil = [
                [q[v, h + 1, 8 * kt + m : 8 * kt + m + 8, :] for m in range(6)] for v in range(NV)
            ]
            pairs = [stencil_pair(x) for x in stencil]
            for v, f in enumerate(face_flux(lambda v: pairs[v][0], lambda v: pairs[v][1], 0)):
                fx[v, h, rows, :] = f
        for kt in range(2):
            rows = slice(8 * kt, 8 * kt + 8)
            cells = slice(8 * kt + 3, 8 * kt + 11)
            rho, pressure = q[0, h + 1, cells, :], q[4, h + 1, cells, :]
            ratio = rho / pressure
            rates = [
                pre[r] * rho * q[5 + r, h + 1, cells, :] * jnp.exp(-act[r] * ratio) for r in range(NR)
            ]
            release = heat[0] * rates[0]
            for r in range(1, NR):
                release = release + heat[r] * rates[r]
            source = [None] * 4 + [release, -rates[0]]
            source += [rates[r - 1] - rates[r] for r in range(1, NR)] + [rates[NR - 1]]
            flux = face_flux(
                lambda v: fs[h, 16 * v + 8 * kt : 16 * v + 8 * kt + 8, 0:128],
                lambda v: fs[h, 16 * v + 8 * kt : 16 * v + 8 * kt + 8, 128:256],
                2,
            )
            for v, f in enumerate(flux):
                above = jnp.where(first, pltpu.roll(f, NZ - 1, 1), pltpu.roll(f, 127, 1))
                x = (f - above) + (fx[v, h, rows, :] - fx[v, h, 8 * kt + 1 : 8 * kt + 9, :])
                if source[v] is not None:
                    x = x + source[v]
                s[v, h, rows, :] = x
        return 0

    lax.fori_loop(0, 2, half, 0)


def row_terms(q, qb, fs, fy, weights):
    split_tile(q, qb, 0)
    split_tile(q, qb, 3)
    for j in range(3):
        x = dot(qb[j], weights[0]) + dot(qb[j + 1], weights[1])
        if j < 2:
            x = x + dot(qb[j + 2], weights[2])
        fs[j] = x

    def tile(j, _):
        for kt in range(2):
            flux = face_flux(
                lambda v: fs[j, 16 * v + 8 * kt : 16 * v + 8 * kt + 8, 0:128],
                lambda v: fs[j, 16 * v + 8 * kt : 16 * v + 8 * kt + 8, 128:256],
                1,
            )
            for v, f in enumerate(flux):
                fy[v, j, 8 * kt : 8 * kt + 8, :] = f
        return 0

    lax.fori_loop(0, 3, tile, 0)


def rate_of(s, fy, v, h, kt):
    rows = slice(8 * kt, 8 * kt + 8)
    f = fy[v, h, rows, :]
    last = lane() >= 96
    above = jnp.where(last, pltpu.roll(fy[v, h + 1, rows, :], 96, 1), pltpu.roll(f, 96, 1))
    return s[v, h, rows, :] + (f - above)


def mirrored(x, sign):
    group = lane() // NZ
    return sign * jnp.where(group % 2 == 0, pltpu.roll(x, 32, 1), pltpu.roll(x, 96, 1))


def kernel(n_gx, n_gy, u, fresh_in, slide, cuts_in, pre_in, act_in, heat_in, out, us, fresh, cuts, pre, act, heat, xw, yl, yh, fb, yf, vw, xs, xl, xg, yl2, yh2,
           q, qb, fs, fx, fy, s, weights, send_sem, recv_sem, load_sem):
    gx, gy = lax.axis_index("gx"), lax.axis_index("gy")
    has_prev, has_next = gx > 0, gx < n_gx - 1
    has_below, has_above = gy > 0, gy < n_gy - 1
    inside = {-1: has_prev, 1: has_next}
    beside = {-1: has_below, 1: has_above}
    pairs = ((u, us), (fresh_in, fresh), (cuts_in, cuts), (pre_in, pre), (act_in, act), (heat_in, heat))
    loads = [pltpu.make_async_copy(a, b, load_sem.at[k]) for k, (a, b) in enumerate(pairs)]

    def both(a, b):
        return jnp.logical_and(a, b)

    def reach(dx, dy):
        if dx and dy:
            return both(inside[dx], beside[dy])
        return inside[dx] if dx else beside[dy]

    neighbours = [(a, b) for a in (-1, 0, 1) for b in (-1, 0, 1) if a or b]
    barrier = pltpu.get_barrier_semaphore()
    for dx, dy in neighbours:

        @pl.when(reach(dx, dy))
        def _(dx=dx, dy=dy):
            pl.semaphore_signal(barrier, inc=1, device_id=(gx + dx, gy + dy), device_id_type=MESH)

    for load in loads:
        load.start()
    for load in loads:
        load.wait()
    base = jnp.clip(cuts[gx] - gx * PX + slide[0], -2, 9)
    count = jnp.clip(cuts[gx + 1] - cuts[gx], 9, CAP)
    for p in range(PX):
        for h in range(2):
            xw[h, OWN + NV * p : OWN + NV * (p + 1), :] = us[p, :, 128 * h : 128 * h + 128]
    for h in range(2):
        fb[h, 0:NV, :] = fresh[:, 128 * h : 128 * h + 128]
        fb[h, NV:16, :] = jnp.zeros((2, 128), jnp.float32)
    along = 1 + jnp.where(has_prev, 1, 0) + jnp.where(has_next, 1, 0)
    across = 1 + jnp.where(has_below, 1, 0) + jnp.where(has_above, 1, 0)
    pl.semaphore_wait(barrier, along * across - 1)

    def remote(k, src, dst, dx, dy):
        return pltpu.make_async_remote_copy(
            src_ref=src, dst_ref=dst, send_sem=send_sem.at[k], recv_sem=recv_sem.at[k],
            device_id=(gx + dx, gy + dy), device_id_type=MESH,
        )

    x_first = [
        (has_prev, remote(0, xw.at[:, OWN:NEXT], xw.at[:, NEXT : NEXT + PX * NV], -1, 0), has_next),
        (has_next, remote(1, xw.at[:, OWN + 96 : NEXT], xw.at[:, 40:OWN], 1, 0), has_prev),
    ]
    y_first = []
    for k, (dy, h, ghost) in enumerate(((1, 1, yl), (-1, 0, yh))):
        to, of = beside[dy], beside[-dy]
        y_first.append((to, remote(2 + 4 * k, xw.at[h, OWN:NEXT], ghost.at[Y_OWN:Y_NEXT], 0, dy), of))
        y_first.append((
            both(to, has_prev),
            remote(3 + 4 * k, xw.at[h, OWN : OWN + 128], ghost.at[Y_NEXT : Y_NEXT + 128], -1, dy),
            both(of, has_next),
        ))
        y_first.append((
            both(to, has_next),
            remote(4 + 4 * k, xw.at[h, OWN + 136 : NEXT], ghost.at[Y_OWN - 32 : Y_OWN], 1, dy),
            both(of, has_prev),
        ))
        y_first.append((
            both(to, jnp.logical_not(has_next)),
            remote(5 + 4 * k, fb.at[h], yf.at[k], 0, dy),
            both(of, jnp.logical_not(has_next)),
        ))

    def start(copies):
        for to, copy, _ in copies:

            @pl.when(to)
            def _(copy=copy):
                copy.start()

    def arrive(copies):
        for _, copy, of in copies:

            @pl.when(of)
            def _(copy=copy):
                copy.wait_recv()

    def leave(copies):
        for to, copy, _ in copies:

            @pl.when(to)
            def _(copy=copy):
                copy.wait_send()

    start(x_first)
    start(y_first)
    fill_weights(weights)
    row_id = lax.broadcasted_iota(jnp.int32, (8, 128), 0)

    arrive(x_first)

    @pl.when(jnp.logical_not(has_next))
    def _():
        for p in range(12, 27):
            for h in range(2):
                xw[h, OWN + NV * p : OWN + NV * (p + 1), :] = fb[h, 0:NV, :]

    def window(h, k, v):
        return xw[h, pl.ds((base + 8 + k) * NV + v, 8, stride=NV), :]

    low_edge = both(jnp.logical_not(has_prev), row_id < 3)

    def window_tile(h, _):
        for j in range(3):
            c = [window(h, 8 * j - 3, v) for v in range(NV)]
            if j == 0:
                c = [jnp.where(low_edge, xw[h, pl.ds((base + 8) * NV + v, 1), :], c[v]) for v in range(NV)]
            store_primitives(q, h + 1, 8 * j, c)
        return 0

    lax.fori_loop(0, 2, window_tile, 0)
    inner_terms(q, qb, fs, fx, s, weights, (pre, act, heat))

    arrive(y_first)

    @pl.when(jnp.logical_not(has_next))
    def _():
        for p in range(12, 21):
            for ghost, k in ((yl, 0), (yh, 1)):
                ghost[Y_OWN + NV * p : Y_OWN + NV * (p + 1), :] = yf[k, 0:NV, :]

    for t, h, ghost, is_wall in ((0, 0, yl, jnp.logical_not(has_below)), (3, 1, yh, jnp.logical_not(has_above))):
        for kt in range(2):

            @pl.when(is_wall)
            def _(t=t, h=h, kt=kt):
                c = [mirrored(window(h, 8 * kt, v), -1.0 if v == 2 else 1.0) for v in range(NV)]
                store_primitives(q, t, 8 * kt + 3, c)

            @pl.when(jnp.logical_not(is_wall))
            def _(t=t, ghost=ghost, kt=kt):
                c = [ghost[pl.ds((base + 4 + 8 * kt) * NV + v, 8, stride=NV), :] for v in range(NV)]
                store_primitives(q, t, 8 * kt + 3, c)

    row_terms(q, qb, fs, fy, weights)

    def first_update(h, _):
        for kt in range(2):
            for v in range(NV):
                x = window(h, 8 * kt, v) + TIME_STEP * rate_of(s, fy, v, h, kt)
                vw[h, pl.ds(V_OWN + 8 * kt * NV + v, 8, stride=NV), :] = x
        return 0

    lax.fori_loop(0, 2, first_update, 0)

    for h in range(2):
        xs[h] = vw[h, pl.ds(V_OWN + (count - 3) * NV - 6, 48), :]
    second = [
        (has_prev, remote(10, vw.at[:, V_OWN : V_OWN + 48], xg.at[:, G_OWN : G_OWN + 48], -1, 0), has_next),
        (has_next, remote(11, xs, xl.at[:, 0:48], 1, 0), has_prev),
    ]
    y_second = [
        (has_above, remote(12, vw.at[1, V_OWN : V_OWN + 216], yl2.at[0:216], 0, 1), has_below),
        (has_below, remote(13, vw.at[0, V_OWN : V_OWN + 216], yh2.at[0:216], 0, -1), has_above),
    ]
    start(second)
    start(y_second)

    @pl.when(jnp.logical_not(has_next))
    def _():
        for p in range(3):
            for h in range(2):
                xg[h, G_OWN + NV * p : G_OWN + NV * (p + 1), :] = fb[h, 0:NV, :]

    arrive(second)

    def second_tile(h, _):
        for j in range(3):
            k = 8 * j - 3
            c = [vw[h, pl.ds(V_OWN + k * NV + v, 8, stride=NV), :] for v in range(NV)]
            if j == 0:
                ghosts = [xl[h, pl.ds(6 + v, 8, stride=NV), :] for v in range(NV)]
                c = [jnp.where(row_id < 3, ghosts[v], c[v]) for v in range(NV)]
                c = [jnp.where(low_edge, vw[h, V_OWN + v : V_OWN + v + 1, :], c[v]) for v in range(NV)]
            else:
                owned = row_id + k < count
                c = [
                    jnp.where(owned, c[v], xg[h, pl.ds(G_OWN + (k - count) * NV + v, 8, stride=NV), :])
                    for v in range(NV)
                ]
            store_primitives(q, h + 1, 8 * j, c)
        return 0

    lax.fori_loop(0, 2, second_tile, 0)
    inner_terms(q, qb, fs, fx, s, weights, (pre, act, heat))

    arrive(y_second)
    for t, h, ghost, is_wall in ((0, 0, yl2, jnp.logical_not(has_below)), (3, 1, yh2, jnp.logical_not(has_above))):
        for kt in range(2):

            @pl.when(is_wall)
            def _(t=t, h=h, kt=kt):
                c = [
                    mirrored(vw[h, pl.ds(V_OWN + 8 * kt * NV + v, 8, stride=NV), :], -1.0 if v == 2 else 1.0)
                    for v in range(NV)
                ]
                store_primitives(q, t, 8 * kt + 3, c)

            @pl.when(jnp.logical_not(is_wall))
            def _(t=t, ghost=ghost, kt=kt):
                c = [ghost[pl.ds(8 * kt * NV + v, 8, stride=NV), :] for v in range(NV)]
                store_primitives(q, t, 8 * kt + 3, c)

    row_terms(q, qb, fs, fy, weights)
    for h in range(2):
        for kt in range(2):
            owned = row_id + 8 * kt < count
            for v in range(NV):
                w = window(h, 8 * kt, v)
                x = vw[h, pl.ds(V_OWN + 8 * kt * NV + v, 8, stride=NV), :] + TIME_STEP * rate_of(s, fy, v, h, kt)
                x = jnp.where(owned, 0.75 * w + 0.25 * x, 0.0)
                if kt == 0:
                    out[v, 0:8, 128 * h : 128 * h + 128] = x
                else:
                    out[v, 8:CAP, 128 * h : 128 * h + 128] = x[0 : CAP - 8]

    leave(x_first)
    leave(y_first)
    leave(second)
    leave(y_second)


def body(n_gx, n_gy, gas_state, inflow, slide_count, cut_list, prefactor, activation, heat_release):
    def f32(*shape):
        return pltpu.VMEM(shape, jnp.float32)

    return pl.pallas_call(
        functools.partial(kernel, n_gx, n_gy),
        out_shape=pltpu.VMEM((NV, CAP, 256), jnp.float32),
        in_specs=[pl.BlockSpec(memory_space=m) for m in [pltpu.HBM] * 2 + [pltpu.SMEM] + [pltpu.HBM] * 4],
        out_specs=pl.BlockSpec(memory_space=pltpu.VMEM),
        scratch_shapes=[
            f32(PX, NV, 256),
            f32(NV, 256),
            pltpu.SMEM((n_gx + 1,), jnp.int32),
            pltpu.SMEM((NR,), jnp.float32),
            pltpu.SMEM((NR,), jnp.float32),
            pltpu.SMEM((NR,), jnp.float32),
            f32(2, W_ROWS, 128),
            f32(Y_ROWS, 128),
            f32(Y_ROWS, 128),
            f32(2, 16, 128),
            f32(2, 16, 128),
            f32(2, V_ROWS, 128),
            f32(2, 48, 128),
            f32(2, 136, 128),
            f32(2, G_ROWS, 128),
            f32(240, 128),
            f32(240, 128),
            f32(NV, 4, 24, 128),
            pltpu.VMEM((4, NV * 16, 256), jnp.bfloat16),
            f32(3, NV * 16, 256),
            f32(NV, 2, 24, 128),
            f32(NV, 3, 16, 128),
            f32(NV, 2, 16, 128),
            pltpu.VMEM((4, 256, 256), jnp.bfloat16),
            pltpu.SemaphoreType.DMA((14,)),
            pltpu.SemaphoreType.DMA((14,)),
            pltpu.SemaphoreType.DMA((6,)),
        ],
        compiler_params=pltpu.CompilerParams(
            collective_id=0, has_side_effects=True, vmem_limit_bytes=32 * 1024 * 1024
        ),
        name="two_stages",
    )(*[
        x if x is slide_count else pltpu.with_memory_space_constraint(x, pltpu.HBM)
        for x in (
            jnp.transpose(gas_state, (1, 0, 2)), inflow, slide_count, cut_list, prefactor, activation, heat_release
        )
    ])


def solution(mesh):
    in_specs = (P(None, "gx", "gy"), P(None, "gy"), P(), P(), P(), P(), P())
    return jax.shard_map(
        functools.partial(body, mesh.shape["gx"], mesh.shape["gy"]),
        mesh=mesh,
        in_specs=in_specs,
        out_specs=P(None, "gx", "gy"),
        check_vma=False,
    )
```

time: 135 us -> 33.4 us (0.25); the launches traced: 133 us -> 33.3 us
  local copies, waits for them, and re-layouts: 47.1 us -> 0.69 us
  starting transfers between devices: 43.9 us -> 0 us
  other arithmetic: 36.1 us -> 0 us
  Pallas kernels: 0 us -> 31.9 us
  between operations: 4.54 us -> 0.66 us
  waiting for transfers between devices: 1.67 us -> 0 us
    ppermute x9 -> x0, starting transfers between devices: 43.9 us -> none  [the longest x5 27.9 us: passed_along(): return lax.ppermute(shard, axis, pairs)]
    pallas_call x0 -> x1, Pallas kernels: none -> 31.9 us  [body(): pl.pallas_call(functools.partial(kernel, n_gx, n_gy), out_shape=pltpu.VME...]
    slice x35 -> x0, local copies, waits for them, and re-layouts: 17 us -> none  [the longest x12 5.47 us: to_primitive(): fractions = conserved[5:] / density]
    unnamed x162 -> x1, local copies, waits for them, and re-layouts: 10 us -> 0.69 us
    mul x46 -> x0, other arithmetic: 8.77 us -> none  [the longest x6 2.63 us: divergence(): 0.5 * jnp.maximum(speed_low, speed_high) * (cons_high - cons_low)]
    div x14 -> x0, other arithmetic: 8.42 us -> none  [the longest x6 6.93 us: reconstruct(): (-3.0 * stencil[1] + 27.0 * stencil[2] + 47.0 * stencil[3] - 13.0 * stenc...]
    reshape x4 -> x0, local copies, waits for them, and re-layouts: 4.94 us -> none  [the longest x2 3.53 us: advance_rate(): y_padded = y_flat.reshape(variables, capacity, row_cells + 6, NZ)]
    rev x4 -> x0, local copies, waits for them, and re-layouts: 4.72 us -> none  [mirror(): return jnp.flip(edge_rows, axis=2) * wall_sign]
  transfers between devices with their start and end apart: 9 -> 0, of which waited for: 2 -> 0; matrix products, arithmetic and copies ran while one was open for 25% -> 0% of each run, Pallas kernels for 0% -> 0%
where the time goes in v1:
time: 33.4 us; the launch traced here: 33.3 us
  Pallas kernels  31.9 us (96%)
  local copies, waits for them, and re-layouts  0.69 us (2%)
  between operations  0.66 us (2%)
    pallas_call x1, Pallas kernels, body(): pl.pallas_call(functools.partial(kernel, n_gx, n_gy), out_shape=pltpu.VME...  31.9 us
    unnamed x1, local copies, waits for them, and re-layouts  0.69 us

profile of v1, /device:TPU:38, one launch (start us, length us, event | category | flops | bytes accessed | tf_op | source)
XLA Modules:
  0.0 33.3 jit_solution(17509862756545686483)
XLA Ops:
  0.7 31.9 %two_stages.1 = f32[14,15,256]{2,1,0:T(8,128)S(1)} custom-call(f32[12,14,256]{2,1,0:T(8,128)} %bitcast.1, f32[14,256]{1,0:T(8,128)} %fresh_in.1, s32[1]{0:T(128)S(6)} %copy.10.slide, s32[129]{0:T(256)} %cuts_in.1, f32[8]{0:T(128)} %pre_in.1, f32[8]{0:T(128)} %act_in.1, f32[8]{0:T(128)} %heat_in.1), custom_call_target="tpu_custom_call" | custom-call | tf_op jit(solution)/shard_map/two_stages/pallas_call | solution.py:434
  32.6 0.7 %copy.9 = f32[14,15,256]{2,1,0:T(8,128)} copy(f32[14,15,256]{2,1,0:T(8,128)S(1)} %two_stages.1) | data formatting | bytes 430080

commit v2 on v1

--- a/solution.py
+++ b/solution.py
@@ -22,6 +22,8 @@
 Y_NEXT = Y_OWN + PX * NV
 V_OWN = 4 * NV
 G_OWN = 12 * NV
+
+PARTS = ((0, 42, 0), (0, 32, 128), (136, 8, 224))
 
 W_ROWS = 560
 Y_ROWS = 424
@@ -196,7 +198,27 @@
     return sign * jnp.where(group % 2 == 0, pltpu.roll(x, 32, 1), pltpu.roll(x, 96, 1))
 
 
-def kernel(n_gx, n_gy, u, fresh_in, slide, cuts_in, pre_in, act_in, heat_in, out, us, fresh, cuts, pre, act, heat, xw, yl, yh, fb, yf, vw, xs, xl, xg, yl2, yh2,
+def pack(src, start, quarter, dst, to, free):
+    group = lax.broadcasted_iota(jnp.int32, (quarter, 128), 1) // NZ
+    last = src(start + 3 * quarter, quarter)
+    for j in range(3):
+        moved = pltpu.roll(last, (32 * (3 - j) if free == 3 else 128 - 32 * (j + 1)), 1)
+        dst[to + j * quarter : to + (j + 1) * quarter, :] = jnp.where(
+            group == free, moved, src(start + j * quarter, quarter)
+        )
+
+
+def unpack(src, start, quarter, dst, to, free):
+    group = lax.broadcasted_iota(jnp.int32, (quarter, 128), 1) // NZ
+    last = jnp.ones((quarter, 128), jnp.float32)
+    for j in range(3):
+        x = src[start + j * quarter : start + (j + 1) * quarter, :]
+        dst[to + j * quarter : to + (j + 1) * quarter, :] = jnp.where(group == free, 1.0, x)
+        last = jnp.where(group == (j if free == 3 else j + 1), pltpu.roll(x, 32 * (j + 1), 1), last)
+    dst[to + 3 * quarter : to + 4 * quarter, :] = last
+
+
+def kernel(n_gx, n_gy, u, fresh_in, slide, cuts_in, pre_in, act_in, heat_in, out, us, fresh, cuts, pre, act, heat, xw, yl, yh, fb, yf, vw, xs, xl, xg, yl2, yh2, ps, yp, ps2, yp2,
            q, qb, fs, fx, fy, s, weights, send_sem, recv_sem, load_sem):
     gx, gy = lax.axis_index("gx"), lax.axis_index("gy")
     has_prev, has_next = gx > 0, gx < n_gx - 1
@@ -234,6 +256,9 @@
     for h in range(2):
         fb[h, 0:NV, :] = fresh[:, 128 * h : 128 * h + 128]
         fb[h, NV:16, :] = jnp.zeros((2, 128), jnp.float32)
+    for k, h in ((0, 1), (1, 0)):
+        for row, quarter, to in PARTS:
+            pack(lambda a, n, h=h: xw[h, a : a + n, :], OWN + row, quarter, ps.at[k], to, 3 * k)
     along = 1 + jnp.where(has_prev, 1, 0) + jnp.where(has_next, 1, 0)
     across = 1 + jnp.where(has_below, 1, 0) + jnp.where(has_above, 1, 0)
     pl.semaphore_wait(barrier, along * across - 1)
@@ -249,22 +274,22 @@
         (has_next, remote(1, xw.at[:, OWN + 96 : NEXT], xw.at[:, 40:OWN], 1, 0), has_prev),
     ]
     y_first = []
-    for k, (dy, h, ghost) in enumerate(((1, 1, yl), (-1, 0, yh))):
+    for k, dy in enumerate((1, -1)):
         to, of = beside[dy], beside[-dy]
-        y_first.append((to, remote(2 + 4 * k, xw.at[h, OWN:NEXT], ghost.at[Y_OWN:Y_NEXT], 0, dy), of))
+        y_first.append((to, remote(2 + 4 * k, ps.at[k, 0:128], yp.at[k, 0:128], 0, dy), of))
         y_first.append((
             both(to, has_prev),
-            remote(3 + 4 * k, xw.at[h, OWN : OWN + 128], ghost.at[Y_NEXT : Y_NEXT + 128], -1, dy),
+            remote(3 + 4 * k, ps.at[k, 128:224], yp.at[k, 128:224], -1, dy),
             both(of, has_next),
         ))
         y_first.append((
             both(to, has_next),
-            remote(4 + 4 * k, xw.at[h, OWN + 136 : NEXT], ghost.at[Y_OWN - 32 : Y_OWN], 1, dy),
+            remote(4 + 4 * k, ps.at[k, 224:248], yp.at[k, 224:248], 1, dy),
             both(of, has_prev),
         ))
         y_first.append((
             both(to, jnp.logical_not(has_next)),
-            remote(5 + 4 * k, fb.at[h], yf.at[k], 0, dy),
+            remote(5 + 4 * k, fb.at[1 - k], yf.at[k], 0, dy),
             both(of, jnp.logical_not(has_next)),
         ))
 
@@ -319,6 +344,9 @@
     inner_terms(q, qb, fs, fx, s, weights, (pre, act, heat))
 
     arrive(y_first)
+    for k, ghost in ((0, yl), (1, yh)):
+        for (_, quarter, row), to in zip(PARTS, (Y_OWN, Y_NEXT, Y_OWN - 32)):
+            unpack(yp.at[k], row, quarter, ghost, to, 3 * k)
 
     @pl.when(jnp.logical_not(has_next))
     def _():
@@ -357,10 +385,12 @@
         (has_next, remote(11, xs, xl.at[:, 0:48], 1, 0), has_prev),
     ]
     y_second = [
-        (has_above, remote(12, vw.at[1, V_OWN : V_OWN + 216], yl2.at[0:216], 0, 1), has_below),
-        (has_below, remote(13, vw.at[0, V_OWN : V_OWN + 216], yh2.at[0:216], 0, -1), has_above),
+        (has_above, remote(12, ps2.at[0], yp2.at[0], 0, 1), has_below),
+        (has_below, remote(13, ps2.at[1], yp2.at[1], 0, -1), has_above),
     ]
     start(second)
+    for k, h in ((0, 1), (1, 0)):
+        pack(lambda a, n, h=h: vw[h, a : a + n, :], V_OWN, 56, ps2.at[k], 0, 3 * k)
     start(y_second)
 
     @pl.when(jnp.logical_not(has_next))
@@ -392,6 +422,8 @@
     inner_terms(q, qb, fs, fx, s, weights, (pre, act, heat))
 
     arrive(y_second)
+    for k, ghost in ((0, yl2), (1, yh2)):
+        unpack(yp2.at[k], 0, 56, ghost, 0, 3 * k)
     for t, h, ghost, is_wall in ((0, 0, yl2, jnp.logical_not(has_below)), (3, 1, yh2, jnp.logical_not(has_above))):
         for kt in range(2):
 
@@ -454,6 +486,10 @@
             f32(2, G_ROWS, 128),
             f32(240, 128),
             f32(240, 128),
+            f32(2, 248, 128),
+            f32(2, 248, 128),
+            f32(2, 168, 128),
+            f32(2, 168, 128),
             f32(NV, 4, 24, 128),
             pltpu.VMEM((4, NV * 16, 256), jnp.bfloat16),
             f32(3, NV * 16, 256),

time: 33.4 us -> 32.5 us (0.973)
  the two profiles are of different devices: /device:TPU:38 before, /device:TPU:22 now
where the time goes in v2:
time: 32.5 us; the launch traced here: 32.4 us
  Pallas kernels  31 us (95%)
  local copies, waits for them, and re-layouts  0.69 us (2%)
  between operations  0.66 us (2%)
    pallas_call x1, Pallas kernels, body(): pl.pallas_call(functools.partial(kernel, n_gx, n_gy), out_shape=pltpu.VME...  31 us
    unnamed x1, local copies, waits for them, and re-layouts  0.69 us

profile of v2, /device:TPU:22, one launch (start us, length us, event | category | flops | bytes accessed | tf_op | source)
XLA Modules:
  0.0 32.4 jit_solution(7539895911400058479)
XLA Ops:
  0.7 31.0 %two_stages.1 = f32[14,15,256]{2,1,0:T(8,128)S(1)} custom-call(f32[12,14,256]{2,1,0:T(8,128)} %bitcast.1, f32[14,256]{1,0:T(8,128)} %fresh_in.1, s32[1]{0:T(128)S(6)} %copy.10.slide, s32[129]{0:T(256)} %cuts_in.1, f32[8]{0:T(128)} %pre_in.1, f32[8]{0:T(128)} %act_in.1, f32[8]{0:T(128)} %heat_in.1), custom_call_target="tpu_custom_call" | custom-call | tf_op jit(solution)/shard_map/two_stages/pallas_call | solution.py:466
  31.7 0.7 %copy.9 = f32[14,15,256]{2,1,0:T(8,128)} copy(f32[14,15,256]{2,1,0:T(8,128)S(1)} %two_stages.1) | data formatting | bytes 430080

commit v3 on v2

--- a/solution.py
+++ b/solution.py
@@ -16,17 +16,22 @@
 GAS_GAMMA = 1.4
 TIME_STEP = 0.025
 
-OWN = 8 * NV
+ORIGIN = 16
+OWN = ORIGIN * NV
 NEXT = OWN + PX * NV
-Y_OWN = 4 * NV
+Y_ORIGIN = 12
+Y_OWN = Y_ORIGIN * NV
 Y_NEXT = Y_OWN + PX * NV
 V_OWN = 4 * NV
 G_OWN = 12 * NV
 
 PARTS = ((0, 42, 0), (0, 32, 128), (136, 8, 224))
-
-W_ROWS = 560
-Y_ROWS = 424
+RUN_PART = (96, 18, 248)
+RUN = 32
+ROW0 = 11
+
+W_ROWS = 672
+Y_ROWS = 544
 V_ROWS = 56 + 24 * NV
 G_ROWS = 352
 
@@ -100,11 +105,12 @@
             weights[slot, 128:256, 128 * side : 128 * side + 128] = w
 
 
-def split_tile(q, qb, t):
-    x = q[:, t, 3:19, :].reshape(NV * 16, 128) * (1.0 / 60.0)
+def split_tile(q, qb, t, row, blocks):
+    size = 8 * blocks
+    x = q[:, t, row : row + size, :].reshape(NV * size, 128) * (1.0 / 60.0)
     top = x.astype(jnp.bfloat16)
-    qb[t, :, 0:128] = top
-    qb[t, :, 128:256] = (x - top.astype(jnp.float32)).astype(jnp.bfloat16)
+    qb[t, 0 : NV * size, 0:128] = top
+    qb[t, 0 : NV * size, 128:256] = (x - top.astype(jnp.float32)).astype(jnp.bfloat16)
 
 
 def dot(a, b):
@@ -116,26 +122,25 @@
         q[v, t, row : row + 8, :] = value
 
 
-def inner_terms(q, qb, fs, fx, s, weights, rate):
+def inner_terms(q, qb, fs, fx, s, weights, rate, row=ROW0, blocks=2):
     pre, act, heat = rate
+    size = 8 * blocks
     for t in (1, 2):
-        split_tile(q, qb, t)
-        fs[t - 1] = dot(qb[t], weights[3])
+        split_tile(q, qb, t, row, blocks)
+        fs[t - 1, 0 : NV * size] = dot(qb[t, 0 : NV * size], weights[3])
     first = lane() % NZ == NZ - 1
 
     def half(h, _):
         for kt in range(2):
-            rows = slice(8 * kt, 8 * kt + 8)
-            cells = slice(8 * kt + 3, 8 * kt + 11)
             stencil = [
-                [q[v, h + 1, 8 * kt + m : 8 * kt + m + 8, :] for m in range(6)] for v in range(NV)
+                [q[v, h + 1, row - 3 + 8 * kt + m : row + 5 + 8 * kt + m, :] for m in range(6)] for v in range(NV)
             ]
             pairs = [stencil_pair(x) for x in stencil]
             for v, f in enumerate(face_flux(lambda v: pairs[v][0], lambda v: pairs[v][1], 0)):
-                fx[v, h, rows, :] = f
-        for kt in range(2):
+                fx[v, h, 8 * kt : 8 * kt + 8, :] = f
+        for kt in range(blocks):
             rows = slice(8 * kt, 8 * kt + 8)
-            cells = slice(8 * kt + 3, 8 * kt + 11)
+            cells = slice(row + 8 * kt, row + 8 * kt + 8)
             rho, pressure = q[0, h + 1, cells, :], q[4, h + 1, cells, :]
             ratio = rho / pressure
             rates = [
@@ -147,8 +152,8 @@
             source = [None] * 4 + [release, -rates[0]]
             source += [rates[r - 1] - rates[r] for r in range(1, NR)] + [rates[NR - 1]]
             flux = face_flux(
-                lambda v: fs[h, 16 * v + 8 * kt : 16 * v + 8 * kt + 8, 0:128],
-                lambda v: fs[h, 16 * v + 8 * kt : 16 * v + 8 * kt + 8, 128:256],
+                lambda v: fs[h, size * v + 8 * kt : size * v + 8 * kt + 8, 0:128],
+                lambda v: fs[h, size * v + 8 * kt : size * v + 8 * kt + 8, 128:256],
                 2,
             )
             for v, f in enumerate(flux):
@@ -162,20 +167,22 @@
     lax.fori_loop(0, 2, half, 0)
 
 
-def row_terms(q, qb, fs, fy, weights):
-    split_tile(q, qb, 0)
-    split_tile(q, qb, 3)
+def row_terms(q, qb, fs, fy, weights, row=ROW0, blocks=2):
+    size = 8 * blocks
+    split_tile(q, qb, 0, row, blocks)
+    split_tile(q, qb, 3, row, blocks)
+    tiles = [qb[t, 0 : NV * size] for t in range(4)]
     for j in range(3):
-        x = dot(qb[j], weights[0]) + dot(qb[j + 1], weights[1])
+        x = dot(tiles[j], weights[0]) + dot(tiles[j + 1], weights[1])
         if j < 2:
-            x = x + dot(qb[j + 2], weights[2])
-        fs[j] = x
+            x = x + dot(tiles[j + 2], weights[2])
+        fs[j, 0 : NV * size] = x
 
     def tile(j, _):
-        for kt in range(2):
+        for kt in range(blocks):
             flux = face_flux(
-                lambda v: fs[j, 16 * v + 8 * kt : 16 * v + 8 * kt + 8, 0:128],
-                lambda v: fs[j, 16 * v + 8 * kt : 16 * v + 8 * kt + 8, 128:256],
+                lambda v: fs[j, size * v + 8 * kt : size * v + 8 * kt + 8, 0:128],
+                lambda v: fs[j, size * v + 8 * kt : size * v + 8 * kt + 8, 128:256],
                 1,
             )
             for v, f in enumerate(flux):
@@ -218,10 +225,12 @@
     dst[to + 3 * quarter : to + 4 * quarter, :] = last
 
 
-def kernel(n_gx, n_gy, u, fresh_in, slide, cuts_in, pre_in, act_in, heat_in, out, us, fresh, cuts, pre, act, heat, xw, yl, yh, fb, yf, vw, xs, xl, xg, yl2, yh2, ps, yp, ps2, yp2,
-           q, qb, fs, fx, fy, s, weights, send_sem, recv_sem, load_sem):
+def kernel(n_gx, n_gy, u, fresh_in, slide, cuts_in, pre_in, act_in, heat_in, out, us, fresh, cuts, pre, act, heat, xw, yl, yh, fb, yf, xe, vw, xs, xl, xg, yl2, yh2, ps, yp, ps2, yp2,
+           q, qb, fs, fx, fy, s, weights, send_sem, recv_sem, load_sem, late_sem):
     gx, gy = lax.axis_index("gx"), lax.axis_index("gy")
     has_prev, has_next = gx > 0, gx < n_gx - 1
+    starts_run = jnp.logical_and(has_prev, lax.rem(gx, RUN) == 0)
+    ends_run = jnp.logical_and(has_next, lax.rem(gx, RUN) == RUN - 1)
     has_below, has_above = gy > 0, gy < n_gy - 1
     inside = {-1: has_prev, 1: has_next}
     beside = {-1: has_below, 1: has_above}
@@ -231,37 +240,35 @@
     def both(a, b):
         return jnp.logical_and(a, b)
 
-    def reach(dx, dy):
-        if dx and dy:
-            return both(inside[dx], beside[dy])
-        return inside[dx] if dx else beside[dy]
-
+    goes_on, went_on = both(has_next, jnp.logical_not(ends_run)), both(has_prev, jnp.logical_not(starts_run))
     neighbours = [(a, b) for a in (-1, 0, 1) for b in (-1, 0, 1) if a or b]
     barrier = pltpu.get_barrier_semaphore()
     for dx, dy in neighbours:
-
-        @pl.when(reach(dx, dy))
+        there = goes_on if dx == 1 else has_prev
+        if dx and dy:
+            there = both(there, beside[dy])
+        elif dy:
+            there = beside[dy]
+
+        @pl.when(there)
         def _(dx=dx, dy=dy):
             pl.semaphore_signal(barrier, inc=1, device_id=(gx + dx, gy + dy), device_id_type=MESH)
 
     for load in loads:
         load.start()
-    for load in loads:
-        load.wait()
-    base = jnp.clip(cuts[gx] - gx * PX + slide[0], -2, 9)
-    count = jnp.clip(cuts[gx + 1] - cuts[gx], 9, CAP)
+    loads[0].wait()
     for p in range(PX):
         for h in range(2):
             xw[h, OWN + NV * p : OWN + NV * (p + 1), :] = us[p, :, 128 * h : 128 * h + 128]
-    for h in range(2):
-        fb[h, 0:NV, :] = fresh[:, 128 * h : 128 * h + 128]
-        fb[h, NV:16, :] = jnp.zeros((2, 128), jnp.float32)
-    for k, h in ((0, 1), (1, 0)):
-        for row, quarter, to in PARTS:
-            pack(lambda a, n, h=h: xw[h, a : a + n, :], OWN + row, quarter, ps.at[k], to, 3 * k)
-    along = 1 + jnp.where(has_prev, 1, 0) + jnp.where(has_next, 1, 0)
+    along = 1 + jnp.where(went_on, 1, 0) + jnp.where(has_next, 1, 0)
     across = 1 + jnp.where(has_below, 1, 0) + jnp.where(has_above, 1, 0)
     pl.semaphore_wait(barrier, along * across - 1)
+    for dy in (-1, 0, 1):
+
+        @pl.when(both(ends_run, beside[dy]) if dy else ends_run)
+        def _(dy=dy):
+            pl.semaphore_signal(late_sem, inc=1, device_id=(gx + 1, gy + dy), device_id_type=MESH)
+
 
     def remote(k, src, dst, dx, dy):
         return pltpu.make_async_remote_copy(
@@ -270,33 +277,31 @@
         )
 
     x_first = [
-        (has_prev, remote(0, xw.at[:, OWN:NEXT], xw.at[:, NEXT : NEXT + PX * NV], -1, 0), has_next),
-        (has_next, remote(1, xw.at[:, OWN + 96 : NEXT], xw.at[:, 40:OWN], 1, 0), has_prev),
+        (has_next, remote(1, xw.at[:, OWN + 96 : NEXT], xw.at[:, OWN - 72 : OWN], 1, 0), has_prev),
     ]
-    y_first = []
+    x_back = [(has_prev, remote(0, xw.at[:, OWN:NEXT], xw.at[:, NEXT : NEXT + PX * NV], -1, 0), has_next)]
+    y_first, y_back = [], []
+    lower = [(ends_run, remote(18, xw.at[:, OWN + 56 : OWN + 96], xe, 1, 0), starts_run)]
     for k, dy in enumerate((1, -1)):
         to, of = beside[dy], beside[-dy]
-        y_first.append((to, remote(2 + 4 * k, ps.at[k, 0:128], yp.at[k, 0:128], 0, dy), of))
-        y_first.append((
-            both(to, has_prev),
-            remote(3 + 4 * k, ps.at[k, 128:224], yp.at[k, 128:224], -1, dy),
-            both(of, has_next),
-        ))
-        y_first.append((
-            both(to, has_next),
-            remote(4 + 4 * k, ps.at[k, 224:248], yp.at[k, 224:248], 1, dy),
-            both(of, has_prev),
-        ))
+        for number, (go, come, dx, a, b) in enumerate((
+            (ends_run, starts_run, 1, 248, 304),
+            (has_prev, has_next, -1, 128, 224),
+            (has_next, has_prev, 1, 224, 248),
+        )):
+            copy = remote(2 + 5 * k + number, ps.at[k, a:b], yp.at[k, a:b], dx, dy)
+            (lower if a == 248 else y_back if dx < 0 else y_first).append((both(to, go), copy, both(of, come)))
+        y_first.append((to, remote(5 + 5 * k, ps.at[k, 0:128], yp.at[k, 0:128], 0, dy), of))
         y_first.append((
             both(to, jnp.logical_not(has_next)),
-            remote(5 + 4 * k, fb.at[1 - k], yf.at[k], 0, dy),
+            remote(6 + 5 * k, fb.at[1 - k], yf.at[k], 0, dy),
             both(of, jnp.logical_not(has_next)),
         ))
 
-    def start(copies):
+    def start(copies, now=True):
         for to, copy, _ in copies:
 
-            @pl.when(to)
+            @pl.when(both(to, now))
             def _(copy=copy):
                 copy.start()
 
@@ -315,10 +320,38 @@
                 copy.wait_send()
 
     start(x_first)
+    start(x_back, went_on)
+    for k, h in ((0, 1), (1, 0)):
+        for row, quarter, to in PARTS:
+            pack(lambda a, n, h=h: xw[h, a : a + n, :], OWN + row, quarter, ps.at[k], to, 3 * k)
+
+    for load in loads[1:]:
+        load.wait()
+    for h in range(2):
+        fb[h, 0:NV, :] = fresh[:, 128 * h : 128 * h + 128]
+        fb[h, NV:16, :] = jnp.zeros((2, 128), jnp.float32)
+    start(y_back, went_on)
     start(y_first)
+
+    @pl.when(ends_run)
+    def _():
+        row, quarter, to = RUN_PART
+        for k, h in ((0, 1), (1, 0)):
+            pack(lambda a, n, h=h: xw[h, a : a + n, :], OWN + row, quarter, ps.at[k], to, 3 * k)
+
+    start(lower)
+    base = jnp.clip(cuts[gx] - gx * PX + slide[0], -2, 9)
+    count = jnp.clip(cuts[gx + 1] - cuts[gx], 9, CAP)
     fill_weights(weights)
     row_id = lax.broadcasted_iota(jnp.int32, (8, 128), 0)
 
+    @pl.when(starts_run)
+    def _():
+        pl.semaphore_wait(late_sem, across)
+
+    start(x_back, starts_run)
+    start(y_back, starts_run)
+    arrive(x_back)
     arrive(x_first)
 
     @pl.when(jnp.logical_not(has_next))
@@ -328,7 +361,7 @@
                 xw[h, OWN + NV * p : OWN + NV * (p + 1), :] = fb[h, 0:NV, :]
 
     def window(h, k, v):
-        return xw[h, pl.ds((base + 8 + k) * NV + v, 8, stride=NV), :]
+        return xw[h, pl.ds((base + ORIGIN + k) * NV + v, 8, stride=NV), :]
 
     low_edge = both(jnp.logical_not(has_prev), row_id < 3)
 
@@ -336,13 +369,14 @@
         for j in range(3):
             c = [window(h, 8 * j - 3, v) for v in range(NV)]
             if j == 0:
-                c = [jnp.where(low_edge, xw[h, pl.ds((base + 8) * NV + v, 1), :], c[v]) for v in range(NV)]
-            store_primitives(q, h + 1, 8 * j, c)
+                c = [jnp.where(low_edge, xw[h, pl.ds((base + ORIGIN) * NV + v, 1), :], c[v]) for v in range(NV)]
+            store_primitives(q, h + 1, 8 * j + 8, c)
         return 0
 
     lax.fori_loop(0, 2, window_tile, 0)
     inner_terms(q, qb, fs, fx, s, weights, (pre, act, heat))
 
+    arrive(y_back)
     arrive(y_first)
     for k, ghost in ((0, yl), (1, yh)):
         for (_, quarter, row), to in zip(PARTS, (Y_OWN, Y_NEXT, Y_OWN - 32)):
@@ -354,18 +388,21 @@
             for ghost, k in ((yl, 0), (yh, 1)):
                 ghost[Y_OWN + NV * p : Y_OWN + NV * (p + 1), :] = yf[k, 0:NV, :]
 
-    for t, h, ghost, is_wall in ((0, 0, yl, jnp.logical_not(has_below)), (3, 1, yh, jnp.logical_not(has_above))):
-        for kt in range(2):
+    def beside_tiles(k):
+        for t, h, ghost, is_wall in ((0, 0, yl, jnp.logical_not(has_below)), (3, 1, yh, jnp.logical_not(has_above))):
 
             @pl.when(is_wall)
-            def _(t=t, h=h, kt=kt):
-                c = [mirrored(window(h, 8 * kt, v), -1.0 if v == 2 else 1.0) for v in range(NV)]
-                store_primitives(q, t, 8 * kt + 3, c)
+            def _(t=t, h=h):
+                c = [mirrored(window(h, k, v), -1.0 if v == 2 else 1.0) for v in range(NV)]
+                store_primitives(q, t, ROW0 + k, c)
 
             @pl.when(jnp.logical_not(is_wall))
-            def _(t=t, ghost=ghost, kt=kt):
-                c = [ghost[pl.ds((base + 4 + 8 * kt) * NV + v, 8, stride=NV), :] for v in range(NV)]
-                store_primitives(q, t, 8 * kt + 3, c)
+            def _(t=t, ghost=ghost):
+                c = [ghost[pl.ds((base + Y_ORIGIN + k) * NV + v, 8, stride=NV), :] for v in range(NV)]
+                store_primitives(q, t, ROW0 + k, c)
+
+    for k in (0, 8):
+        beside_tiles(k)
 
     row_terms(q, qb, fs, fy, weights)
 
@@ -381,12 +418,12 @@
     for h in range(2):
         xs[h] = vw[h, pl.ds(V_OWN + (count - 3) * NV - 6, 48), :]
     second = [
-        (has_prev, remote(10, vw.at[:, V_OWN : V_OWN + 48], xg.at[:, G_OWN : G_OWN + 48], -1, 0), has_next),
-        (has_next, remote(11, xs, xl.at[:, 0:48], 1, 0), has_prev),
+        (has_prev, remote(12, vw.at[:, V_OWN : V_OWN + 48], xg.at[:, G_OWN : G_OWN + 48], -1, 0), has_next),
+        (goes_on, remote(13, xs, xl.at[:, 0:48], 1, 0), went_on),
     ]
     y_second = [
-        (has_above, remote(12, ps2.at[0], yp2.at[0], 0, 1), has_below),
-        (has_below, remote(13, ps2.at[1], yp2.at[1], 0, -1), has_above),
+        (has_above, remote(14, ps2.at[0], yp2.at[0], 0, 1), has_below),
+        (has_below, remote(15, ps2.at[1], yp2.at[1], 0, -1), has_above),
     ]
     start(second)
     for k, h in ((0, 1), (1, 0)):
@@ -398,6 +435,32 @@
         for p in range(3):
             for h in range(2):
                 xg[h, G_OWN + NV * p : G_OWN + NV * (p + 1), :] = fb[h, 0:NV, :]
+
+    arrive(lower)
+
+    @pl.when(starts_run)
+    def _():
+        for h in range(2):
+            xw[h, OWN - 112 : OWN - 72, :] = xe[h]
+        for k, ghost in ((0, yl), (1, yh)):
+            unpack(yp.at[k], RUN_PART[2], RUN_PART[1], ghost, Y_OWN - 72, 3 * k)
+
+        def lower_tile(h, _):
+            store_primitives(q, h + 1, 0, [window(h, -ROW0, v) for v in range(NV)])
+            return 0
+
+        lax.fori_loop(0, 2, lower_tile, 0)
+        beside_tiles(-8)
+        inner_terms(q, qb, fs, fx, s, weights, (pre, act, heat), ROW0 - 8, 1)
+        row_terms(q, qb, fs, fy, weights, ROW0 - 8, 1)
+
+        def lower_update(h, _):
+            for v in range(NV):
+                x = window(h, -8, v) + TIME_STEP * rate_of(s, fy, v, h, 0)
+                xl[h, pl.ds(6 + v, 3, stride=NV), :] = x[5:8]
+            return 0
+
+        lax.fori_loop(0, 2, lower_update, 0)
 
     arrive(second)
 
@@ -415,7 +478,7 @@
                     jnp.where(owned, c[v], xg[h, pl.ds(G_OWN + (k - count) * NV + v, 8, stride=NV), :])
                     for v in range(NV)
                 ]
-            store_primitives(q, h + 1, 8 * j, c)
+            store_primitives(q, h + 1, 8 * j + 8, c)
         return 0
 
     lax.fori_loop(0, 2, second_tile, 0)
@@ -433,12 +496,12 @@
                     mirrored(vw[h, pl.ds(V_OWN + 8 * kt * NV + v, 8, stride=NV), :], -1.0 if v == 2 else 1.0)
                     for v in range(NV)
                 ]
-                store_primitives(q, t, 8 * kt + 3, c)
+                store_primitives(q, t, ROW0 + 8 * kt, c)
 
             @pl.when(jnp.logical_not(is_wall))
             def _(t=t, ghost=ghost, kt=kt):
                 c = [ghost[pl.ds(8 * kt * NV + v, 8, stride=NV), :] for v in range(NV)]
-                store_primitives(q, t, 8 * kt + 3, c)
+                store_primitives(q, t, ROW0 + 8 * kt, c)
 
     row_terms(q, qb, fs, fy, weights)
     for h in range(2):
@@ -453,6 +516,9 @@
                 else:
                     out[v, 8:CAP, 128 * h : 128 * h + 128] = x[0 : CAP - 8]
 
+    leave(lower)
+    leave(x_back)
+    leave(y_back)
     leave(x_first)
     leave(y_first)
     leave(second)
@@ -480,26 +546,28 @@
             f32(Y_ROWS, 128),
             f32(2, 16, 128),
             f32(2, 16, 128),
+            f32(2, 40, 128),
             f32(2, V_ROWS, 128),
             f32(2, 48, 128),
             f32(2, 136, 128),
             f32(2, G_ROWS, 128),
             f32(240, 128),
             f32(240, 128),
-            f32(2, 248, 128),
-            f32(2, 248, 128),
+            f32(2, 304, 128),
+            f32(2, 304, 128),
             f32(2, 168, 128),
             f32(2, 168, 128),
-            f32(NV, 4, 24, 128),
+            f32(NV, 4, 32, 128),
             pltpu.VMEM((4, NV * 16, 256), jnp.bfloat16),
             f32(3, NV * 16, 256),
             f32(NV, 2, 24, 128),
             f32(NV, 3, 16, 128),
             f32(NV, 2, 16, 128),
             pltpu.VMEM((4, 256, 256), jnp.bfloat16),
-            pltpu.SemaphoreType.DMA((14,)),
-            pltpu.SemaphoreType.DMA((14,)),
+            pltpu.SemaphoreType.DMA((19,)),
+            pltpu.SemaphoreType.DMA((19,)),
             pltpu.SemaphoreType.DMA((6,)),
+            pltpu.SemaphoreType.REGULAR,
         ],
         compiler_params=pltpu.CompilerParams(
             collective_id=0, has_side_effects=True, vmem_limit_bytes=32 * 1024 * 1024

time: 32.5 us -> 29.7 us (0.914)
  the two profiles are of different devices: /device:TPU:22 before, /device:TPU:6 now
where the time goes in v3:
time: 29.7 us; the launch traced here: 29.6 us
  Pallas kernels  28.2 us (95%)
  local copies, waits for them, and re-layouts  0.69 us (2%)
  between operations  0.66 us (2%)
    pallas_call x1, Pallas kernels, body(): pl.pallas_call(functools.partial(kernel, n_gx, n_gy), out_shape=pltpu.VME...  28.2 us
    unnamed x1, local copies, waits for them, and re-layouts  0.69 us

profile of v3, /device:TPU:6, one launch (start us, length us, event | category | flops | bytes accessed | tf_op | source)
XLA Modules:
  0.0 29.6 jit_solution(2304048092684580385)
XLA Ops:
  0.7 28.2 %two_stages.1 = f32[14,15,256]{2,1,0:T(8,128)S(1)} custom-call(f32[12,14,256]{2,1,0:T(8,128)} %bitcast.1, f32[14,256]{1,0:T(8,128)} %fresh_in.1, s32[1]{0:T(128)S(6)} %copy.10.slide, s32[129]{0:T(256)} %cuts_in.1, f32[8]{0:T(128)} %pre_in.1, f32[8]{0:T(128)} %act_in.1, f32[8]{0:T(128)} %heat_in.1), custom_call_target="tpu_custom_call" | custom-call | tf_op jit(solution)/shard_map/two_stages/pallas_call | solution.py:532
  28.9 0.7 %copy.9 = f32[14,15,256]{2,1,0:T(8,128)} copy(f32[14,15,256]{2,1,0:T(8,128)S(1)} %two_stages.1) | data formatting | bytes 430080

commit v4 on v3

--- a/solution.py
+++ b/solution.py
@@ -26,7 +26,7 @@
 G_OWN = 12 * NV
 
 PARTS = ((0, 42, 0), (0, 32, 128), (136, 8, 224))
-RUN_PART = (96, 18, 248)
+RUN_PART = (96, 11, 248)
 RUN = 32
 ROW0 = 11
 
@@ -127,7 +127,12 @@
     size = 8 * blocks
     for t in (1, 2):
         split_tile(q, qb, t, row, blocks)
-        fs[t - 1, 0 : NV * size] = dot(qb[t, 0 : NV * size], weights[3])
+    x, y = qb[1, 0 : NV * size], qb[2, 0 : NV * size]
+    fs[0, 0 : NV * size] = dot(x, weights[3])
+    fs[1, 0 : NV * size] = dot(y, weights[3])
+    fs[2, 0 : NV * size] = dot(x, weights[1]) + dot(y, weights[2])
+    fs[3, 0 : NV * size] = dot(x, weights[0]) + dot(y, weights[1])
+    fs[4, 0 : NV * size] = dot(y, weights[0])
     first = lane() % NZ == NZ - 1
 
     def half(h, _):
@@ -171,18 +176,16 @@
     size = 8 * blocks
     split_tile(q, qb, 0, row, blocks)
     split_tile(q, qb, 3, row, blocks)
-    tiles = [qb[t, 0 : NV * size] for t in range(4)]
-    for j in range(3):
-        x = dot(tiles[j], weights[0]) + dot(tiles[j + 1], weights[1])
-        if j < 2:
-            x = x + dot(tiles[j + 2], weights[2])
-        fs[j, 0 : NV * size] = x
+    x, y = qb[0, 0 : NV * size], qb[3, 0 : NV * size]
+    fs[2, 0 : NV * size] += dot(x, weights[0])
+    fs[3, 0 : NV * size] += dot(y, weights[2])
+    fs[4, 0 : NV * size] += dot(y, weights[1])
 
     def tile(j, _):
         for kt in range(blocks):
             flux = face_flux(
-                lambda v: fs[j, size * v + 8 * kt : size * v + 8 * kt + 8, 0:128],
-                lambda v: fs[j, size * v + 8 * kt : size * v + 8 * kt + 8, 128:256],
+                lambda v: fs[j + 2, size * v + 8 * kt : size * v + 8 * kt + 8, 0:128],
+                lambda v: fs[j + 2, size * v + 8 * kt : size * v + 8 * kt + 8, 128:256],
                 1,
             )
             for v, f in enumerate(flux):
@@ -280,17 +283,17 @@
         (has_next, remote(1, xw.at[:, OWN + 96 : NEXT], xw.at[:, OWN - 72 : OWN], 1, 0), has_prev),
     ]
     x_back = [(has_prev, remote(0, xw.at[:, OWN:NEXT], xw.at[:, NEXT : NEXT + PX * NV], -1, 0), has_next)]
-    y_first, y_back = [], []
+    y_first, y_back, y_near = [], [], []
     lower = [(ends_run, remote(18, xw.at[:, OWN + 56 : OWN + 96], xe, 1, 0), starts_run)]
     for k, dy in enumerate((1, -1)):
         to, of = beside[dy], beside[-dy]
         for number, (go, come, dx, a, b) in enumerate((
-            (ends_run, starts_run, 1, 248, 304),
+            (ends_run, starts_run, 1, 248, 288),
             (has_prev, has_next, -1, 128, 224),
             (has_next, has_prev, 1, 224, 248),
         )):
             copy = remote(2 + 5 * k + number, ps.at[k, a:b], yp.at[k, a:b], dx, dy)
-            (lower if a == 248 else y_back if dx < 0 else y_first).append((both(to, go), copy, both(of, come)))
+            (lower if a == 248 else y_back if dx < 0 else y_near).append((both(to, go), copy, both(of, come)))
         y_first.append((to, remote(5 + 5 * k, ps.at[k, 0:128], yp.at[k, 0:128], 0, dy), of))
         y_first.append((
             both(to, jnp.logical_not(has_next)),
@@ -319,27 +322,31 @@
             def _(copy=copy):
                 copy.wait_send()
 
+    def pack_part(part):
+        row, quarter, to = part
+        for k, h in ((0, 1), (1, 0)):
+            pack(lambda a, n, h=h: xw[h, a : a + n, :], OWN + row, quarter, ps.at[k], to, 3 * k)
+
     start(x_first)
-    start(x_back, went_on)
-    for k, h in ((0, 1), (1, 0)):
-        for row, quarter, to in PARTS:
-            pack(lambda a, n, h=h: xw[h, a : a + n, :], OWN + row, quarter, ps.at[k], to, 3 * k)
-
+    pack_part(PARTS[2])
+    start(y_near)
+    start(lower[:1])
+
+    @pl.when(ends_run)
+    def _():
+        pack_part(RUN_PART)
+
+    start(lower[1:])
+    pack_part(PARTS[1])
+    start(y_back, went_on)
+    pack_part(PARTS[0])
     for load in loads[1:]:
         load.wait()
     for h in range(2):
         fb[h, 0:NV, :] = fresh[:, 128 * h : 128 * h + 128]
         fb[h, NV:16, :] = jnp.zeros((2, 128), jnp.float32)
-    start(y_back, went_on)
     start(y_first)
-
-    @pl.when(ends_run)
-    def _():
-        row, quarter, to = RUN_PART
-        for k, h in ((0, 1), (1, 0)):
-            pack(lambda a, n, h=h: xw[h, a : a + n, :], OWN + row, quarter, ps.at[k], to, 3 * k)
-
-    start(lower)
+    start(x_back, went_on)
     base = jnp.clip(cuts[gx] - gx * PX + slide[0], -2, 9)
     count = jnp.clip(cuts[gx + 1] - cuts[gx], 9, CAP)
     fill_weights(weights)
@@ -377,6 +384,7 @@
     inner_terms(q, qb, fs, fx, s, weights, (pre, act, heat))
 
     arrive(y_back)
+    arrive(y_near)
     arrive(y_first)
     for k, ghost in ((0, yl), (1, yh)):
         for (_, quarter, row), to in zip(PARTS, (Y_OWN, Y_NEXT, Y_OWN - 32)):
@@ -520,6 +528,7 @@
     leave(x_back)
     leave(y_back)
     leave(x_first)
+    leave(y_near)
     leave(y_first)
     leave(second)
     leave(y_second)
@@ -553,13 +562,13 @@
             f32(2, G_ROWS, 128),
             f32(240, 128),
             f32(240, 128),
-            f32(2, 304, 128),
-            f32(2, 304, 128),
+            f32(2, 288, 128),
+            f32(2, 288, 128),
             f32(2, 168, 128),
             f32(2, 168, 128),
             f32(NV, 4, 32, 128),
             pltpu.VMEM((4, NV * 16, 256), jnp.bfloat16),
-            f32(3, NV * 16, 256),
+            f32(5, NV * 16, 256),
             f32(NV, 2, 24, 128),
             f32(NV, 3, 16, 128),
             f32(NV, 2, 16, 128),

time: 29.7 us -> 28.5 us (0.960)
  Pallas kernels: 28.2 us -> 27 us
    pallas_call x1, Pallas kernels: 28.2 us -> 27 us  [body(): pl.pallas_call(functools.partial(kernel, n_gx, n_gy), out_shape=pltpu.VME...]
where the time goes in v4:
time: 28.5 us; the launch traced here: 28.4 us
  Pallas kernels  27 us (95%)
  local copies, waits for them, and re-layouts  0.69 us (2%)
  between operations  0.66 us (2%)
    pallas_call x1, Pallas kernels, body(): pl.pallas_call(functools.partial(kernel, n_gx, n_gy), out_shape=pltpu.VME...  27 us
    unnamed x1, local copies, waits for them, and re-layouts  0.69 us

profile of v4, /device:TPU:6, one launch (start us, length us, event | category | flops | bytes accessed | tf_op | source)
XLA Modules:
  0.0 28.4 jit_solution(6818056350666155890)
XLA Ops:
  0.7 27.0 %two_stages.1 = f32[14,15,256]{2,1,0:T(8,128)S(1)} custom-call(f32[12,14,256]{2,1,0:T(8,128)} %bitcast.1, f32[14,256]{1,0:T(8,128)} %fresh_in.1, s32[1]{0:T(128)S(6)} %copy.10.slide, s32[129]{0:T(256)} %cuts_in.1, f32[8]{0:T(128)} %pre_in.1, f32[8]{0:T(128)} %act_in.1, f32[8]{0:T(128)} %heat_in.1), custom_call_target="tpu_custom_call" | custom-call | tf_op jit(solution)/shard_map/two_stages/pallas_call | solution.py:541
  27.7 0.7 %copy.9 = f32[14,15,256]{2,1,0:T(8,128)} copy(f32[14,15,256]{2,1,0:T(8,128)S(1)} %two_stages.1) | data formatting | bytes 430080

commit v5 on v4

--- a/solution.py
+++ b/solution.py
@@ -414,29 +414,24 @@
 
     row_terms(q, qb, fs, fy, weights)
 
-    def first_update(h, _):
+    y_second = [
+        (has_above, remote(14, ps2.at[0], yp2.at[0], 0, 1), has_below),
+        (has_below, remote(15, ps2.at[1], yp2.at[1], 0, -1), has_above),
+    ]
+    for k, h in ((0, 1), (1, 0)):
         for kt in range(2):
             for v in range(NV):
                 x = window(h, 8 * kt, v) + TIME_STEP * rate_of(s, fy, v, h, kt)
                 vw[h, pl.ds(V_OWN + 8 * kt * NV + v, 8, stride=NV), :] = x
-        return 0
-
-    lax.fori_loop(0, 2, first_update, 0)
-
+        pack(lambda a, n, h=h: vw[h, a : a + n, :], V_OWN, 56, ps2.at[k], 0, 3 * k)
+        start(y_second[k : k + 1])
     for h in range(2):
         xs[h] = vw[h, pl.ds(V_OWN + (count - 3) * NV - 6, 48), :]
     second = [
         (has_prev, remote(12, vw.at[:, V_OWN : V_OWN + 48], xg.at[:, G_OWN : G_OWN + 48], -1, 0), has_next),
         (goes_on, remote(13, xs, xl.at[:, 0:48], 1, 0), went_on),
     ]
-    y_second = [
-        (has_above, remote(14, ps2.at[0], yp2.at[0], 0, 1), has_below),
-        (has_below, remote(15, ps2.at[1], yp2.at[1], 0, -1), has_above),
-    ]
     start(second)
-    for k, h in ((0, 1), (1, 0)):
-        pack(lambda a, n, h=h: vw[h, a : a + n, :], V_OWN, 56, ps2.at[k], 0, 3 * k)
-    start(y_second)
 
     @pl.when(jnp.logical_not(has_next))
     def _():

time: 28.5 us -> 28.5 us (level)
  no operation moved by 1% of the time
where the time goes in v5:
time: 28.5 us; the launch traced here: 28.4 us
  Pallas kernels  27 us (95%)
  local copies, waits for them, and re-layouts  0.69 us (2%)
  between operations  0.66 us (2%)
    pallas_call x1, Pallas kernels, body(): pl.pallas_call(functools.partial(kernel, n_gx, n_gy), out_shape=pltpu.VME...  27 us
    unnamed x1, local copies, waits for them, and re-layouts  0.69 us

profile of v5, /device:TPU:6, one launch (start us, length us, event | category | flops | bytes accessed | tf_op | source)
XLA Modules:
  0.0 28.4 jit_solution(5169019139607046150)
XLA Ops:
  0.7 27.0 %two_stages.1 = f32[14,15,256]{2,1,0:T(8,128)S(1)} custom-call(f32[12,14,256]{2,1,0:T(8,128)} %bitcast.1, f32[14,256]{1,0:T(8,128)} %fresh_in.1, s32[1]{0:T(128)S(6)} %copy.10.slide, s32[129]{0:T(256)} %cuts_in.1, f32[8]{0:T(128)} %pre_in.1, f32[8]{0:T(128)} %act_in.1, f32[8]{0:T(128)} %heat_in.1), custom_call_target="tpu_custom_call" | custom-call | tf_op jit(solution)/shard_map/two_stages/pallas_call | solution.py:536
  27.7 0.7 %copy.9 = f32[14,15,256]{2,1,0:T(8,128)} copy(f32[14,15,256]{2,1,0:T(8,128)S(1)} %two_stages.1) | data formatting | bytes 430080
